TPU v7x, 512 devices: a whole 4x4x16 slice. The times are simulated.
512 devices in a mesh: tensor: 16 (over y, z_hi), context: 32 (over x, z_lo, core).
Axes of the slice: x: 4, y: 4, z: 16 (z_hi: 4, z_lo: 4; z = z_hi * 4 + z_lo), core: 2. Of those that a mesh axis runs over, the one named last changes fastest.
Arguments:
- projected: bfloat16 [3, 8192, 4096], P(None, 'tensor', 'context'), may hold values from -6 to 6
- short_weight: float32 [3, 8192, 3], P(None, 'tensor'), may hold values from -3.5 to 3.5
- residues: float32 [8192, 16], P(('tensor', 'context')), may hold values from -1.5 to 1.5
- decay_rates: float32 [8192, 16], P(('tensor', 'context')), may hold values from 0.5 to 128
- skip_weight: float32 [8192], P(('tensor', 'context')), may hold values from -3 to 3
- cotangent: bfloat16 [8192, 4096], P('tensor', 'context'), may hold values from -6 to 6
Outputs:
- output: bfloat16 [8192, 4096], P('tensor', 'context')
- grad_projected: bfloat16 [3, 8192, 4096], P(None, 'tensor', 'context')
- grad_short: float32 [3, 8192, 3], P(None, 'tensor')
- grad_residues: float32 [8192, 16], P(('tensor', 'context'))
- grad_decay: float32 [8192, 16], P(('tensor', 'context'))
- grad_skip: float32 [8192], P(('tensor', 'context'))
All inputs are finite; a program needn't handle non-finite values.
Results may differ from a plain program's by a relative error of at most 0.0062.
Values may be sent and summed in bfloat16 or wider, within the bound.
A program may use at most 64 MiB of HBM per device.

v0:
```python
import math

import jax
import jax.numpy as jnp
from jax import lax
from jax.sharding import PartitionSpec as P

PRECISE = lax.Precision.HIGH


def passed_along(block, axis, distance):
    devices = range(lax.axis_size(axis))
    route = [(i - distance, i) for i in devices if i - distance in devices]
    return lax.ppermute(block, axis, route)


def mode_terms(decay_rates, length):
    per_step = decay_rates / length
    scales = jnp.sqrt(-jnp.expm1(-2.0 * per_step))
    return (per_step, scales)


def filter_taps(residues, per_step, scales, length):
    times = jnp.arange(length).astype(jnp.float32)
    coefs = residues * scales

    def add_mode(index, total):
        rate_col = lax.dynamic_slice_in_dim(per_step, index, 1, 1)
        coef_col = lax.dynamic_slice_in_dim(coefs, index, 1, 1)
        return total + coef_col * jnp.exp(-rate_col * times[None, :])

    start = jnp.zeros((residues.shape[0], length), jnp.float32)
    return lax.fori_loop(0, residues.shape[1], add_mode, start)


def mode_grads(grad_filter, residues, per_step, scales, length):
    times = jnp.arange(length).astype(jnp.float32)
    rates_rows = per_step.T

    def one_mode(rate_row):
        weights = jnp.exp(-rate_row[:, None] * times[None, :])
        plain = jnp.sum(grad_filter * weights, axis=1)
        ramped = jnp.sum(grad_filter * weights * times[None, :], axis=1)
        return jnp.stack([plain, ramped])

    sums = lax.map(one_mode, rates_rows)
    plain = sums[:, 0, :].T
    ramped = sums[:, 1, :].T
    root = math.sqrt(length)
    grad_residues = scales * plain / root
    grad_decay = (
        residues * (jnp.exp(-2.0 * per_step) / scales * plain - scales * ramped) / (length * root)
    )
    return (grad_residues, grad_decay)


def dft_tables(length):
    total = 2 * length
    outer = 128
    inner = total // outer
    half_rows = outer // 2
    row_index = jnp.arange(outer, dtype=jnp.int32)
    col_index = jnp.arange(inner, dtype=jnp.int32)
    full_turn = 2.0 * math.pi
    outer_angle = (
        full_turn
        * (row_index[:, None] * row_index[None, :half_rows] % outer).astype(jnp.float32)
        / outer
    )
    twist_angle = (
        full_turn * (row_index[:, None] * col_index[None, :] % total).astype(jnp.float32) / total
    )
    inner_angle = (
        full_turn * (col_index[:, None] * col_index[None, :] % inner).astype(jnp.float32) / inner
    )
    return (
        jnp.cos(outer_angle),
        jnp.sin(outer_angle),
        jnp.cos(twist_angle),
        jnp.sin(twist_angle),
        jnp.cos(inner_angle),
        jnp.sin(inner_angle),
    )


def inner_product(left, table):
    return jnp.einsum("ckb,bm->ckm", left, table, precision=PRECISE)


def forward_dft(signal, tables):
    cos_outer, sin_outer, cos_twist, sin_twist, cos_inner, sin_inner = tables
    channels = signal.shape[0]
    blocks = signal.reshape(channels, cos_outer.shape[1], cos_inner.shape[0])
    real_part = jnp.einsum("ka,cab->ckb", cos_outer, blocks, precision=PRECISE)
    imag_part = -jnp.einsum("ka,cab->ckb", sin_outer, blocks, precision=PRECISE)
    turned_re = real_part * cos_twist + imag_part * sin_twist
    turned_im = imag_part * cos_twist - real_part * sin_twist
    spec_re = inner_product(turned_re, cos_inner) + inner_product(turned_im, sin_inner)
    spec_im = inner_product(turned_im, cos_inner) - inner_product(turned_re, sin_inner)
    return (spec_re, spec_im)


def inverse_dft(spectrum, tables):
    cos_outer, sin_outer, cos_twist, sin_twist, cos_inner, sin_inner = tables
    spec_re, spec_im = spectrum
    channels = spec_re.shape[0]
    middle_re = inner_product(spec_re, cos_inner) - inner_product(spec_im, sin_inner)
    middle_im = inner_product(spec_im, cos_inner) + inner_product(spec_re, sin_inner)
    turned_re = middle_re * cos_twist - middle_im * sin_twist
    turned_im = middle_im * cos_twist + middle_re * sin_twist
    blocks = jnp.einsum("ka,ckb->cab", cos_outer, turned_re, precision=PRECISE)
    blocks = blocks - jnp.einsum("ka,ckb->cab", sin_outer, turned_im, precision=PRECISE)
    total = cos_outer.shape[0] * cos_inner.shape[0]
    return blocks.reshape(channels, -1) / total


def complex_times(left, right):
    return (left[0] * right[0] - left[1] * right[1], left[0] * right[1] + left[1] * right[0])


def conjugate(value):
    return (value[0], -value[1])


def convolve(gated_ch, spec_taps, skip_weight, tables):
    gated_float = gated_ch.astype(jnp.float32)
    spec_gated = forward_dft(gated_float, tables)
    conv_ch = (
        inverse_dft(complex_times(spec_gated, spec_taps), tables)
        + skip_weight[:, None] * gated_float
    )
    return (conv_ch.astype(jnp.bfloat16), spec_gated, gated_float)


def correlate(
    grad_ch,
    gated_float,
    spec_gated,
    spec_taps,
    residues,
    per_step,
    scales,
    skip_weight,
    tables,
    length,
):
    grad_float = grad_ch.astype(jnp.float32)
    spec_grad = forward_dft(grad_float, tables)
    back_ch = (
        inverse_dft(complex_times(spec_grad, conjugate(spec_taps)), tables)
        + skip_weight[:, None] * grad_float
    )
    grad_filter = inverse_dft(complex_times(spec_grad, conjugate(spec_gated)), tables)
    grad_skip = jnp.sum(grad_float * gated_float, axis=1) / math.sqrt(length)
    grad_res, grad_dec = mode_grads(grad_filter, residues, per_step, scales, length)
    return (back_ch.astype(jnp.bfloat16), grad_res, grad_dec, grad_skip)


def per_device(projected, short_weight, residues, decay_rates, skip_weight, cotangent):
    local_len = projected.shape[2]
    tap_count = short_weight.shape[2]
    length = local_len * lax.axis_size("context")
    rim_before = passed_along(projected[:, :, local_len - tap_count + 1 :], "context", 1)
    extended = jnp.concatenate([rim_before, projected], axis=2).astype(jnp.float32)
    filtered = jnp.zeros(projected.shape, jnp.float32)
    for offset in range(tap_count):
        start = tap_count - 1 - offset
        filtered = (
            filtered
            + short_weight[:, :, offset : offset + 1] * extended[:, :, start : start + local_len]
        )
    query_path = filtered[0]
    key_path = filtered[1]
    value_path = filtered[2]
    gated_signal = (key_path * value_path).astype(jnp.bfloat16)
    cot_float = cotangent.astype(jnp.float32)
    grad_conv = (cot_float * query_path).astype(jnp.bfloat16)
    tables = dft_tables(length)
    per_step, scales = mode_terms(decay_rates, length)
    spec_taps = forward_dft(filter_taps(residues, per_step, scales, length), tables)
    gated_ch = lax.all_to_all(gated_signal, "context", split_axis=0, concat_axis=1, tiled=True)
    conv_ch, spec_gated, gated_float = convolve(gated_ch, spec_taps, skip_weight, tables)
    conv_out = lax.all_to_all(conv_ch, "context", split_axis=1, concat_axis=0, tiled=True)
    grad_ch = lax.all_to_all(grad_conv, "context", split_axis=0, concat_axis=1, tiled=True)
    back_ch, grad_res, grad_dec, grad_skip = correlate(
        grad_ch,
        gated_float,
        spec_gated,
        spec_taps,
        residues,
        per_step,
        scales,
        skip_weight,
        tables,
        length,
    )
    grad_signal = lax.all_to_all(back_ch, "context", split_axis=1, concat_axis=0, tiled=True)
    conv_float = conv_out.astype(jnp.float32)
    output = (query_path * conv_float).astype(jnp.bfloat16)
    signal_float = grad_signal.astype(jnp.float32)
    grad_filtered = jnp.stack(
        [cot_float * conv_float, signal_float * value_path, signal_float * key_path]
    )
    rim_after = passed_along(grad_filtered[:, :, : tap_count - 1], "context", -1)
    padded_grad = jnp.concatenate([grad_filtered, rim_after], axis=2)
    grad_projected = jnp.zeros(grad_filtered.shape, jnp.float32)
    for offset in range(tap_count):
        grad_projected = (
            grad_projected
            + short_weight[:, :, offset : offset + 1]
            * padded_grad[:, :, offset : offset + local_len]
        )
    grad_projected = grad_projected.astype(jnp.bfloat16)
    columns = []
    for offset in range(tap_count):
        start = tap_count - 1 - offset
        columns.append(jnp.sum(grad_filtered * extended[:, :, start : start + local_len], axis=2))
    partial_taps = jnp.stack(columns, axis=2)
    grad_short = lax.psum(partial_taps, "context") / math.sqrt(length)
    return (output, grad_projected, grad_short, grad_res, grad_dec, grad_skip)


def solution(mesh):
    return jax.shard_map(
        per_device,
        mesh=mesh,
        in_specs=(
            P(None, "tensor", "context"),
            P(None, "tensor", None),
            P(("tensor", "context"), None),
            P(("tensor", "context"), None),
            P(("tensor", "context")),
            P("tensor", "context"),
        ),
        out_specs=(
            P("tensor", "context"),
            P(None, "tensor", "context"),
            P(None, "tensor", None),
            P(("tensor", "context"), None),
            P(("tensor", "context"), None),
            P(("tensor", "context")),
        ),
        check_vma=False,
    )
```

profile of v0, /device:TPU:1, one launch (start us, length us, event | category | flops | bytes accessed | tf_op | source)
XLA Modules:
  0.0 248.9 jit_solution(8933142500192374688)
XLA Ops:
  1.8 4.9 %collective-permute-start = (bf16[3,512,2]{2,1,0:T(8,128)(2,1)S(1)}, bf16[3,512,2]{2,1,0:T(8,128)(2,1)}, u32[]{:S(2)}, u32[]{:S(2)}) collective-permute-start(bf16[3,512,2]{2,1,0:T(8,128)(2,1)S(1)} %slice.77), channel_id=1, source_target_pairs={{0,1},{1,2},{2,3},{3,4},{4,5},{5,6},{6,7},{7,8},{8,9},{9,10},{10,1... | collective-permute-start | bytes 18440 | tf_op jit(solution)/shard_map/ppermute | solution.py:14
  8.5 2.9 %while.27 = (s32[]{:T(128)}, f32[16,4096]{1,0:T(8,128)S(1)}, f32[16,16]{0,1:T(8,128)S(1)}, f32[16,16]{0,1:T(8,128)S(1)}, s32[]{:T(128)}, /*index=5*/s32[]{:T(128)}) while((s32[]{:T(128)}, f32[16,4096]{1,0:T(8,128)S(1)}, f32[16,16]{0,1:T(8,128)S(1)}, f32[16,16]{0,1:T(8,128)S(1)}, s32[]{:T(128)}, /*index=5*/s32[]{:T(128)}) %tuple.88), condition=%wide.region_1.2_spmd.clone, body=%wide.region_0.1_spmd.clone.sunk | while | flops 266259 | bytes 557523 | solution.py:33
  19.5 8.2 %all-to-all-start = ((bf16[32,16,128]{2,1,0:T(8,128)(2,1)}), bf16[32,16,128]{2,1,0:T(8,128)(2,1)}, u32[]{:S(2)}, u32[]{:S(2)}) async-start(bf16[32,16,128]{2,1,0:T(8,128)(2,1)} %bitcast.199), calls=%async_computation | async-start | bytes 262144 | tf_op jit(solution)/shard_map/all_to_all | solution.py:181
  27.7 2.4 convolution_subtract_fusion.7
  30.8 5.8 %all-to-all-done = bf16[32,16,128]{2,1,0:T(8,128)(2,1)} async-done(((bf16[32,16,128]{2,1,0:T(8,128)(2,1)}), bf16[32,16,128]{2,1,0:T(8,128)(2,1)}, u32[]{:S(2)}, u32[]{:S(2)}) %all-to-all-start) | async-done | bytes 131104 | tf_op jit(solution)/shard_map/all_to_all | solution.py:181
  36.5 4.7 %all-to-all-start.2 = ((bf16[32,16,128]{2,1,0:T(8,128)(2,1)}), bf16[32,16,128]{2,1,0:T(8,128)(2,1)}, u32[]{:S(2)}, u32[]{:S(2)}) async-start(bf16[32,16,128]{2,1,0:T(8,128)(2,1)} %bitcast.16), calls=%async_computation.2 | async-start | bytes 262144 | tf_op jit(solution)/shard_map/all_to_all | solution.py:184
  47.7 2.2 all-to-all-done.2
  50.0 1.6 copy.59
  51.5 1.7 reshape.125
  54.7 1.4 fusion.8
  68.1 2.1 copy.62
  70.2 1.9 div.196
  76.3 2.2 copy.57
  78.4 1.9 div.193
  80.3 2.3 fusion.47
  82.6 5.6 %all-to-all-start.3 = ((bf16[16,32,128]{2,0,1:T(8,128)(2,1)}), bf16[16,32,128]{2,0,1:T(8,128)(2,1)}, u32[]{:S(2)}, u32[]{:S(2)}) async-start(bf16[16,32,128]{2,0,1:T(8,128)(2,1)} %get-tuple-element.245), calls=%async_computation.3 | async-start | bytes 262144 | tf_op jit(solution)/shard_map/all_to_all | solution.py:197
  91.7 5.4 %all-to-all-done.3 = bf16[16,32,128]{2,0,1:T(8,128)(2,1)} async-done(((bf16[16,32,128]{2,0,1:T(8,128)(2,1)}), bf16[16,32,128]{2,0,1:T(8,128)(2,1)}, u32[]{:S(2)}, u32[]{:S(2)}) %all-to-all-start.3) | async-done | bytes 131104 | tf_op jit(solution)/shard_map/all_to_all | solution.py:197
  97.0 4.0 %all-to-all-start.1 = ((bf16[16,32,128]{2,0,1:T(8,128)(2,1)}), bf16[16,32,128]{2,0,1:T(8,128)(2,1)S(1)}, u32[]{:S(2)}, u32[]{:S(2)}) async-start(bf16[16,32,128]{2,0,1:T(8,128)(2,1)} %get-tuple-element.244), calls=%async_computation.1 | async-start | bytes 262144 | tf_op jit(solution)/shard_map/all_to_all | solution.py:183
  101.1 5.1 %while.26 = (s32[]{:T(128)}, f32[16,2,16]{2,1,0:T(2,128)S(1)}, f32[16,16]{1,0:T(8,128)S(1)}, f32[16,4096]{1,0:T(8,128)S(1)}, s32[]{:T(128)}) while((s32[]{:T(128)}, f32[16,2,16]{2,1,0:T(2,128)S(1)}, f32[16,16]{1,0:T(8,128)S(1)}, f32[16,4096]{1,0:T(8,128)S(1)}, s32[]{:T(128)}) %tuple.91), condition=%wide.region_9.10_spmd.clone.clone, body=%wide.region_6.9_spmd.clone.clone.sunk | while | flops 331794 | bytes 297349 | solution.py:46
  107.9 2.0 all-to-all-done.1
  110.9 2.3 collective-permute-start.1
  113.7 2.2 collective-permute-done.1
  116.3 2.9 %multiply_reduce_fusion.3 = (f32[3,512]{1,0:T(4,128)S(1)}, f32[3,512]{1,0:T(4,128)S(1)}, f32[3,512]{1,0:T(4,128)S(1)}, bf16[3,512,128]{2,1,0:T(8,128)(2,1)}) fusion(f32[3,512,130]{2,1,0:T(8,128)S(1)} %maximum_convert_fusion, f32[1,512,128]{2,1,0:T(8,128)S(1)} %get-tuple-element.241, f32[1,512,128]{2,1,0:T(8,128)S(1)} %get-tuple-element.240, ...), kind=kLoop, calls=%fused_computation.55 | loop fusion | flops 2747904 | bytes 5148672 | tf_op jit(solution)/shard_map/reduce_sum | solution.py:217
  119.3 128.9 %psum.7 = f32[3,512,3]{1,0,2:T(4,128)S(1)} all-reduce(f32[3,512,3]{1,0,2:T(4,128)S(1)} %pad_maximum_fusion.2), channel_id=1, replica_groups=mesh['tensor'=16,'context'=32] {'context'}, use_global_device_ids=true, to_apply=%region_5.6 | all-reduce | flops 4608 | bytes 36864 | tf_op jit(solution)/shard_map/psum | solution.py:219
  (208 shorter events, 50.0 us)
Async XLA Ops:
  1.8 14.5 %collective-permute-start = (bf16[3,512,2]{2,1,0:T(8,128)(2,1)S(1)}, bf16[3,512,2]{2,1,0:T(8,128)(2,1)}, u32[]{:S(2)}, u32[]{:S(2)}) collective-permute-start(bf16[3,512,2]{2,1,0:T(8,128)(2,1)S(1)} %slice.77), channel_id=1, source_target_pairs={{0,1},{1,2},{2,3},{3,4},{4,5},{5,6},{6,7},{7,8},{8,9},{9,10},{10,1... | collective-permute-start | bytes 18440 | tf_op jit(solution)/shard_map/ppermute | solution.py:14
  13.0 1.9 copy-start.12
  13.5 2.7 %copy-start.7 = (bf16[3,512,128]{2,1,0:T(8,128)(2,1)S(1)}, bf16[3,512,128]{2,1,0:T(8,128)(2,1)}, u32[]{:S(2)}) copy-start(bf16[3,512,128]{2,1,0:T(8,128)(2,1)} %param.10) | copy-start | bytes 1179652
  19.5 17.0 %all-to-all-start = ((bf16[32,16,128]{2,1,0:T(8,128)(2,1)}), bf16[32,16,128]{2,1,0:T(8,128)(2,1)}, u32[]{:S(2)}, u32[]{:S(2)}) async-start(bf16[32,16,128]{2,1,0:T(8,128)(2,1)} %bitcast.199), calls=%async_computation | async-start | bytes 262144 | tf_op jit(solution)/shard_map/all_to_all | solution.py:181
  27.6 2.4 copy-start.8
  36.5 13.4 %all-to-all-start.2 = ((bf16[32,16,128]{2,1,0:T(8,128)(2,1)}), bf16[32,16,128]{2,1,0:T(8,128)(2,1)}, u32[]{:S(2)}, u32[]{:S(2)}) async-start(bf16[32,16,128]{2,1,0:T(8,128)(2,1)} %bitcast.16), calls=%async_computation.2 | async-start | bytes 262144 | tf_op jit(solution)/shard_map/all_to_all | solution.py:184
  42.3 0.7 copy-start.2
  56.2 1.1 copy-start.6
  56.7 1.1 copy-start.5
  58.4 1.0 copy-start.3
  58.4 1.2 copy-start.4
  74.9 5.4 %copy-start.13 = (f32[16]{0:T(128)S(1)}, f32[16]{0:T(128)}, u32[]{:S(2)}) copy-start(f32[16]{0:T(128)} %param.14) | copy-start | bytes 196
  76.3 12.0 %copy-start = (f32[16,128,64]{1,2,0:T(8,128)S(1)}, f32[16,128,64]{1,2,0:T(8,128)}, u32[]{:S(2)}) copy-start(f32[16,128,64]{1,2,0:T(8,128)} %convolution_subtract_fusion.1) | copy-start | bytes 1572868
  76.3 12.0 %copy-start.1 = (f32[16,128,64]{1,2,0:T(8,128)S(1)}, f32[16,128,64]{1,2,0:T(8,128)}, u32[]{:S(2)}) copy-start(f32[16,128,64]{1,2,0:T(8,128)} %convolution_add_fusion) | copy-start | bytes 1572868
  82.6 14.4 %all-to-all-start.3 = ((bf16[16,32,128]{2,0,1:T(8,128)(2,1)}), bf16[16,32,128]{2,0,1:T(8,128)(2,1)}, u32[]{:S(2)}, u32[]{:S(2)}) async-start(bf16[16,32,128]{2,0,1:T(8,128)(2,1)} %get-tuple-element.245), calls=%async_computation.3 | async-start | bytes 262144 | tf_op jit(solution)/shard_map/all_to_all | solution.py:197
  91.4 14.9 %copy-start.10 = (f32[16,16]{1,0:T(8,128)S(1)}, f32[16,16]{1,0:T(8,128)}, u32[]{:S(2)}) copy-start(f32[16,16]{1,0:T(8,128)} %param.13) | copy-start | bytes 3076
  91.5 14.8 %copy-start.11 = (f32[16,16]{1,0:T(8,128)S(1)}, f32[16,16]{1,0:T(8,128)}, u32[]{:S(2)}) copy-start(f32[16,16]{1,0:T(8,128)} %param.12) | copy-start | bytes 3076
  97.0 12.9 %copy-start.9 = (bf16[512,128]{1,0:T(8,128)(2,1)S(1)}, bf16[512,128]{1,0:T(8,128)(2,1)}, u32[]{:S(2)}) copy-start(bf16[512,128]{1,0:T(8,128)(2,1)} %param.15) | copy-start | bytes 393220
  97.0 12.9 %all-to-all-start.1 = ((bf16[16,32,128]{2,0,1:T(8,128)(2,1)}), bf16[16,32,128]{2,0,1:T(8,128)(2,1)S(1)}, u32[]{:S(2)}, u32[]{:S(2)}) async-start(bf16[16,32,128]{2,0,1:T(8,128)(2,1)} %get-tuple-element.244), calls=%async_computation.1 | async-start | bytes 262144 | tf_op jit(solution)/shard_map/all_to_all | solution.py:183
  110.9 5.0 %collective-permute-start.1 = (f32[3,512,2]{1,2,0:T(2,128)S(1)}, f32[3,512,2]{1,2,0:T(2,128)S(1)}, u32[]{:S(2)}, u32[]{:S(2)}) collective-permute-start(f32[3,512,2]{1,2,0:T(2,128)S(1)} %copy.64), channel_id=1, source_target_pairs={{1,0},{2,1},{3,2},{4,3},{5,4},{6,5},{7,6},{8,7},{9,8},{10,9},{11,1... | collective-permute-start | bytes 36872 | tf_op jit(solution)/shard_map/ppermute | solution.py:14
where the time goes:
time: 254 us; the launch traced here: 249 us
  blocking collectives  129 us (51%)
  matrix products  31.6 us (12%)
  starting transfers between devices  29.8 us (12%)
  other arithmetic  20 us (8%)
  local copies, waits for them, and re-layouts  18.7 us (7%)
  waiting for transfers between devices  17.6 us (7%)
    psum x1, blocking collectives, per_device(): grad_short = lax.psum(partial_taps, 'context') / math.sqrt(length)  129 us
    dot_general x24, matrix products, inner_product(): return jnp.einsum('ckb,bm->ckm', left, table, precision=PRECISE)  19.7 us
    div x6, local copies, waits for them, and re-layouts, inverse_dft(): return blocks.reshape(channels, -1) / total  9.41 us
    all_to_all x1, starting transfers between devices, per_device(): lax.all_to_all(gated_signal, 'context', split_axis=0, concat_axis=1, tile...  8.15 us
    ppermute x2, starting transfers between devices, passed_along(): return lax.ppermute(block, axis, route)  7.24 us
    all_to_all x1, waiting for transfers between devices, per_device(): lax.all_to_all(gated_signal, 'context', split_axis=0, concat_axis=1, tile...  5.76 us
    all_to_all x1, starting transfers between devices, per_device(): lax.all_to_all(back_ch, 'context', split_axis=1, concat_axis=0, tiled=True)  5.62 us
    all_to_all x1, waiting for transfers between devices, per_device(): lax.all_to_all(back_ch, 'context', split_axis=1, concat_axis=0, tiled=True)  5.37 us
  transfers between devices with their start and end apart: 6, of which 5 were waited for; matrix products, arithmetic and copies ran while one was open for 11% of the time, Pallas kernels for 0%

commit v1 on v0

v1 whole, which is shorter than its diff:
```python
import functools
import math

import jax
import jax.numpy as jnp
from jax import lax
from jax.experimental import pallas as pl
from jax.experimental.pallas import tpu as pltpu
from jax.sharding import PartitionSpec as P

MESH = pl.DeviceIdType.MESH
SUB = 8
MODES = 16
TAPS = 3
OFF = 8
F32 = jnp.float32


def rounded(value):
    return value.astype(jnp.bfloat16).astype(F32)


def one_minus_exp(x):
    series = jnp.ones_like(x)
    for k in range(10, 1, -1):
        series = 1.0 - x * (1.0 / k) * series
    return jnp.where(x < 0.5, x * series, 1.0 - jnp.exp(-x))


def kernel(
    n,
    local_len,
    own,
    proj_ref,
    cot_ref,
    sw_ref,
    decay_ref,
    res_ref,
    skip_ref,
    out_ref,
    gproj_ref,
    gshort_ref,
    gres_ref,
    gdec_ref,
    gskip_ref,
    rx,
    xt,
    qs,
    ks,
    vs,
    us,
    gs,
    ys,
    zs,
    gf,
    ot,
    so,
    gsend,
    grecv,
    par,
    wt,
    lam,
    coef,
    tots,
    sin,
    pacc,
    racc,
    send_sem,
    recv_sem,
    own_sem,
):
    me = lax.axis_index("context")
    length = n * local_len
    steps = local_len // SUB
    groups = 128 // own
    tiles = n // groups
    root = math.sqrt(length)

    def peer_at(t):
        return lax.rem(me + t, n)

    def each_peer(body):
        def step(t, carry):
            body(peer_at(t))
            return carry

        lax.fori_loop(1, n, step, 0)

    barrier = pltpu.get_barrier_semaphore()
    each_peer(
        lambda p: pl.semaphore_signal(
            barrier, inc=1, device_id={"context": p}, device_id_type=MESH
        )
    )

    lane = lax.broadcasted_iota(jnp.int32, (1, 128), 1)
    group = lane // own
    sub_row = lax.broadcasted_iota(jnp.int32, (SUB, 128), 0)

    def spread(row):
        row = jnp.where(lane < own, row, 0.0)
        width = own
        while width < 128:
            row = row + pltpu.roll(row, width, 1)
            width *= 2
        return row

    def group_sum(rows):
        width = own
        while width < 128:
            rows = rows + pltpu.roll(rows, width, 1)
            width *= 2
        return rows

    par[...] = jnp.zeros_like(par)
    for g in range(groups):
        par[0, g * own : (g + 1) * own, 0:MODES] = decay_ref[...]
        par[1, g * own : (g + 1) * own, 0:MODES] = res_ref[...]
    per = par[0].T[0:MODES, :] * (1.0 / length)
    residue = par[1].T[0:MODES, :]
    scale = jnp.sqrt(one_minus_exp(2.0 * per))
    coef_rows = residue * scale
    lam_rows = jnp.exp(-per)
    par[2, 0:MODES, :] = per
    for m in range(MODES):
        lam[m] = jnp.broadcast_to(lam_rows[m : m + 1, :], (SUB, 128))
        coef[m] = jnp.broadcast_to(coef_rows[m : m + 1, :], (SUB, 128))
    first_lane = pl.multiple_of((me // groups) * 128, 128)
    shift = lax.rem(128 - lax.rem(me, groups) * own, 128)
    for i in range(3):
        rows = pltpu.roll(
            jnp.concatenate(
                [sw_ref[i, :, pl.ds(first_lane, 128)], jnp.zeros((SUB - TAPS, 128), F32)], axis=0
            ),
            shift,
            1,
        )
        for j in range(TAPS):
            wt[TAPS * i + j] = jnp.broadcast_to(spread(rows[j : j + 1, :]), (SUB, 128))
    par[3, 0:1, 0:own] = skip_ref[...]
    wt[9] = jnp.broadcast_to(spread(par[3, 0:1, :]), (SUB, 128))

    pl.semaphore_wait(barrier, n - 1)

    def send_inputs(p):
        rows = pl.ds(pl.multiple_of(p * own, own), own)
        pltpu.make_async_remote_copy(
            src_ref=proj_ref.at[:, rows, :],
            dst_ref=rx.at[me, pl.ds(0, 3)],
            send_sem=send_sem.at[0],
            recv_sem=recv_sem.at[0],
            device_id={"context": p},
            device_id_type=MESH,
        ).start()
        pltpu.make_async_remote_copy(
            src_ref=cot_ref.at[rows, :],
            dst_ref=rx.at[me, 3],
            send_sem=send_sem.at[1],
            recv_sem=recv_sem.at[1],
            device_id={"context": p},
            device_id_type=MESH,
        ).start()

    each_peer(send_inputs)
    my_rows = pl.ds(pl.multiple_of(me * own, own), own)
    keep_proj = pltpu.make_async_copy(
        proj_ref.at[:, my_rows, :], rx.at[me, pl.ds(0, 3)], own_sem.at[0]
    )
    keep_cot = pltpu.make_async_copy(cot_ref.at[my_rows, :], rx.at[me, 3], own_sem.at[1])
    keep_proj.start()
    keep_cot.start()
    keep_proj.wait()
    keep_cot.wait()
    others = pl.ds(0, n - 1)
    all_proj = rx.at[others, pl.ds(0, 3)]
    all_cot = rx.at[others, 3]
    pltpu.make_async_copy(all_proj, all_proj, recv_sem.at[0]).wait()
    pltpu.make_async_copy(all_cot, all_cot, recv_sem.at[1]).wait()

    def turn(jt, carry):
        for a in range(4):
            block = rx[pl.ds(groups * jt, groups), a].reshape(128, local_len).astype(F32)
            xt[a, jt, OFF : OFF + local_len, :] = block.T
        return carry

    lax.fori_loop(0, tiles, turn, 0)
    for a in range(3):
        for jt in range(tiles):
            before = pltpu.roll(xt[a, jt, OFF + local_len - 8 : OFF + local_len, :], own, 1)
            if jt:
                last = pltpu.roll(xt[a, jt - 1, OFF + local_len - 8 : OFF + local_len, :], own, 1)
            else:
                last = jnp.zeros((8, 128), F32)
            xt[a, jt, 0:8, :] = jnp.where(group == 0, last, before)

    def gates(jt, carry):
        for p in range(steps):
            paths = []
            for a in range(3):
                total = None
                for j in range(TAPS):
                    rows = xt[a, jt, pl.ds(OFF + p - j, SUB, stride=steps), :]
                    term = wt[TAPS * a + j] * rows
                    total = term if total is None else total + term
                paths.append(total)
            query, key, value = paths
            qs[jt, p] = query
            ks[jt, p] = key
            vs[jt, p] = value
            us[jt, p] = rounded(key * value)
            gs[jt, p] = rounded(xt[3, jt, pl.ds(OFF + p, SUB, stride=steps), :] * query)
        return carry

    lax.fori_loop(0, tiles, gates, 0)

    many = 4

    def ends(at, carry):
        jt = at // (MODES // many)
        first = lax.rem(at, MODES // many) * many
        lams = [lam[first + i] for i in range(many)]
        fwd = [None] * many
        bwd = [None] * many
        for p in range(steps):
            u = us[jt, p]
            g = gs[jt, steps - 1 - p]
            for i in range(many):
                fwd[i] = u if fwd[i] is None else lams[i] * fwd[i] + u
                bwd[i] = g if bwd[i] is None else lams[i] * bwd[i] + g
        for i in range(many):
            pers = jnp.broadcast_to(par[2, pl.ds(first + i, 1), :], (SUB, 128))
            f, b = fwd[i], bwd[i]
            for k in (1, 2, 4):
                factor = jnp.exp(pers * (-1.0 * steps * k))
                f = f + factor * jnp.where(sub_row >= k, pltpu.roll(f, k, 0), 0.0)
                b = b + factor * jnp.where(sub_row < SUB - k, pltpu.roll(b, SUB - k, 0), 0.0)
            sin[0, jt, first + i] = f
            sin[1, jt, first + i] = b
            tots[0, jt, pl.ds(first + i, 1), :] = f[SUB - 1 : SUB, :]
            tots[1, jt, pl.ds(first + i, 1), :] = b[0:1, :]
        return carry

    lax.fori_loop(0, tiles * (MODES // many), ends, 0)

    per_all = par[2, 0:MODES, :]
    spans = [jnp.exp(per_all * (-1.0 * local_len * k)) for k in (1, 2, 4)]
    tile_span = jnp.exp(per_all * (-1.0 * local_len * groups))
    up_span = jnp.exp(per_all * (-1.0 * local_len) * group.astype(F32))
    down_span = jnp.exp(per_all * (-1.0 * local_len) * (groups - 1 - group).astype(F32))
    carry_f = jnp.zeros((MODES, 128), F32)
    for jt in range(tiles):
        f = tots[0, jt]
        for k, span in zip((1, 2, 4), spans):
            f = f + span * jnp.where(group >= k, pltpu.roll(f, own * k, 1), 0.0)
        before = jnp.where(group >= 1, pltpu.roll(f, own, 1), 0.0)
        tots[0, jt] = before + up_span * carry_f
        last = group_sum(jnp.where(group == groups - 1, f, 0.0))
        carry_f = tile_span * carry_f + last
    carry_b = jnp.zeros((MODES, 128), F32)
    for jt in reversed(range(tiles)):
        b = tots[1, jt]
        for k, span in zip((1, 2, 4), spans):
            b = b + span * jnp.where(group < groups - k, pltpu.roll(b, 128 - own * k, 1), 0.0)
        after = jnp.where(group < groups - 1, pltpu.roll(b, 128 - own, 1), 0.0)
        tots[1, jt] = after + down_span * carry_b
        head = group_sum(jnp.where(group == 0, b, 0.0))
        carry_b = tile_span * carry_b + head

    ys[...] = jnp.zeros_like(ys)
    zs[...] = jnp.zeros_like(zs)
    pacc[...] = jnp.zeros_like(pacc)
    racc[...] = jnp.zeros_like(racc)
    pair = 2

    def modes(at, carry):
        jt = at // (MODES // pair)
        first = lax.rem(at, MODES // pair) * pair
        lams, coefs, f_in, b_in = [], [], [], []
        for i in range(pair):
            m = first + i
            pers = jnp.broadcast_to(par[2, pl.ds(m, 1), :], (SUB, 128))
            sub_f = sub_row.astype(F32)
            f = sin[0, jt, m]
            b = sin[1, jt, m]
            f = jnp.where(sub_row >= 1, pltpu.roll(f, 1, 0), 0.0) + jnp.exp(
                pers * (-1.0 * steps) * sub_f
            ) * jnp.broadcast_to(tots[0, jt, pl.ds(m, 1), :], (SUB, 128))
            b = jnp.where(sub_row < SUB - 1, pltpu.roll(b, SUB - 1, 0), 0.0) + jnp.exp(
                pers * (-1.0 * steps) * (SUB - 1 - sub_f)
            ) * jnp.broadcast_to(tots[1, jt, pl.ds(m, 1), :], (SUB, 128))
            f_in.append(f)
            b_in.append(b)
            lams.append(lam[m])
            coefs.append(coef[m])
        behind = [[None] * (steps + 1) for _ in range(pair)]
        for i in range(pair):
            behind[i][steps] = b_in[i]
        for p in reversed(range(steps)):
            g = gs[jt, p]
            z = zs[jt, p]
            for i in range(pair):
                now = lams[i] * behind[i][p + 1] + g
                behind[i][p] = now
                z = z + coefs[i] * now
            zs[jt, p] = z
        plain = [None] * pair
        ramped = [None] * pair
        state = f_in
        for p in range(steps):
            u = us[jt, p]
            g = gs[jt, p]
            y = ys[jt, p]
            for i in range(pair):
                state[i] = lams[i] * state[i] + u
                y = y + coefs[i] * state[i]
                flat = g * state[i]
                ramp = behind[i][p + 1] * state[i]
                plain[i] = flat if plain[i] is None else plain[i] + flat
                ramped[i] = ramp if ramped[i] is None else ramped[i] + ramp
            ys[jt, p] = y
        for i in range(pair):
            pacc[first + i] += plain[i]
            racc[first + i] += ramped[i]
        return carry

    lax.fori_loop(0, tiles * (MODES // pair), modes, 0)

    def paths_grads(jt, skip_total):
        skip = wt[9]
        for p in range(steps):
            u = us[jt, p]
            g = gs[jt, p]
            conv = rounded(ys[jt, p] + skip * u)
            back = rounded(zs[jt, p] + skip * g)
            at = pl.ds(p, SUB, stride=steps)
            ot[0, jt, at, :] = qs[jt, p] * conv
            gf[0, jt, at, :] = xt[3, jt, pl.ds(OFF + p, SUB, stride=steps), :] * conv
            gf[1, jt, at, :] = back * vs[jt, p]
            gf[2, jt, at, :] = back * ks[jt, p]
            skip_total = skip_total + u * g
        return skip_total

    skip_total = lax.fori_loop(0, tiles, paths_grads, jnp.zeros((SUB, 128), F32))
    for a in range(3):
        for jt in range(tiles):
            after = pltpu.roll(gf[a, jt, 0:8, :], 128 - own, 1)
            if jt + 1 < tiles:
                head = pltpu.roll(gf[a, jt + 1, 0:8, :], 128 - own, 1)
            else:
                head = jnp.zeros((8, 128), F32)
            gf[a, jt, local_len : local_len + 8, :] = jnp.where(group == groups - 1, head, after)

    def finish(jt, carry):
        so[pl.ds(groups * jt, groups), 0] = (
            ot[0, jt].T.astype(jnp.bfloat16).reshape(groups, own, local_len)
        )
        totals = []
        for a in range(3):
            total = None
            for j in range(TAPS):
                w = jnp.broadcast_to(wt[TAPS * a + j][0:1, :], (local_len, 128))
                term = w * gf[a, jt, j : j + local_len, :]
                total = term if total is None else total + term
                totals.append(
                    carry[TAPS * a + j]
                    + jnp.sum(
                        gf[a, jt, 0:local_len, :] * xt[a, jt, OFF - j : OFF - j + local_len, :],
                        axis=0,
                        keepdims=True,
                    )
                )
            so[pl.ds(groups * jt, groups), 1 + a] = (
                total.T.astype(jnp.bfloat16).reshape(groups, own, local_len)
            )
        return tuple(totals)

    short = lax.fori_loop(0, tiles, finish, tuple(jnp.zeros((1, 128), F32) for _ in range(9)))
    mine = group == lax.rem(me, groups)
    gsend[...] = jnp.zeros_like(gsend)
    for r in range(9):
        gsend[r : r + 1, :] = jnp.where(mine, group_sum(short[r]), 0.0) * (1.0 / root)

    def send_results(p):
        pltpu.make_async_remote_copy(
            src_ref=so.at[p, 0],
            dst_ref=out_ref.at[my_rows, :],
            send_sem=send_sem.at[2],
            recv_sem=recv_sem.at[2],
            device_id={"context": p},
            device_id_type=MESH,
        ).start()
        pltpu.make_async_remote_copy(
            src_ref=so.at[p, pl.ds(1, 3)],
            dst_ref=gproj_ref.at[:, my_rows, :],
            send_sem=send_sem.at[3],
            recv_sem=recv_sem.at[3],
            device_id={"context": p},
            device_id_type=MESH,
        ).start()
        pltpu.make_async_remote_copy(
            src_ref=gsend,
            dst_ref=grecv.at[me],
            send_sem=send_sem.at[4],
            recv_sem=recv_sem.at[4],
            device_id={"context": p},
            device_id_type=MESH,
        ).start()

    each_peer(send_results)
    keep_out = pltpu.make_async_copy(so.at[me, 0], out_ref.at[my_rows, :], own_sem.at[0])
    keep_gp = pltpu.make_async_copy(
        so.at[me, pl.ds(1, 3)], gproj_ref.at[:, my_rows, :], own_sem.at[1]
    )
    keep_out.start()
    keep_gp.start()
    grecv[me] = gsend[...]

    plain = jnp.concatenate(
        [jnp.sum(pacc[m], axis=0, keepdims=True) for m in range(MODES)], axis=0
    )
    ramped = jnp.concatenate(
        [jnp.sum(racc[m], axis=0, keepdims=True) for m in range(MODES)], axis=0
    )
    plain = group_sum(plain)
    ramped = lam_rows * group_sum(ramped)
    grad_res = scale * plain / root
    grad_dec = (
        residue * (jnp.exp(-2.0 * per_all) / scale * plain - scale * ramped) / (length * root)
    )
    par[0, 0:MODES, :] = grad_res
    par[1, 0:MODES, :] = grad_dec
    gres_ref[...] = par[0].T[0:own, 0:MODES]
    gdec_ref[...] = par[1].T[0:own, 0:MODES]
    gskip_ref[...] = (
        group_sum(jnp.sum(skip_total, axis=0, keepdims=True))[:, 0:own] * (1.0 / root)
    )

    pltpu.make_async_copy(grecv.at[others], grecv.at[others], recv_sem.at[4]).wait()
    for jt in range(tiles):
        total = grecv[groups * jt]
        for g in range(1, groups):
            total = total + grecv[groups * jt + g]
        for i in range(3):
            gshort_ref[i, :, 128 * jt : 128 * (jt + 1)] = total[TAPS * i : TAPS * (i + 1), :]
    keep_out.wait()
    keep_gp.wait()
    most = pl.ds(0, (n - 1) * own)
    pltpu.make_async_copy(out_ref.at[most, :], out_ref.at[most, :], recv_sem.at[2]).wait()
    pltpu.make_async_copy(
        gproj_ref.at[:, most, :], gproj_ref.at[:, most, :], recv_sem.at[3]
    ).wait()
    pltpu.make_async_copy(all_proj, all_proj, send_sem.at[0]).wait()
    pltpu.make_async_copy(all_cot, all_cot, send_sem.at[1]).wait()
    pltpu.make_async_copy(so.at[others, 0], so.at[others, 0], send_sem.at[2]).wait()
    sent = so.at[others, pl.ds(1, 3)]
    pltpu.make_async_copy(sent, sent, send_sem.at[3]).wait()
    pltpu.make_async_copy(grecv.at[others], grecv.at[others], send_sem.at[4]).wait()


def per_device(projected, short_weight, residues, decay_rates, skip_weight, cotangent):
    n = lax.axis_size("context")
    channels, local_len = cotangent.shape
    own = channels // n
    tiles = n // (128 // own)
    steps = local_len // SUB
    vmem = pl.BlockSpec(memory_space=pltpu.VMEM)
    anywhere = pl.BlockSpec(memory_space=pl.ANY)
    stepped = pltpu.VMEM((tiles, steps, SUB, 128), F32)
    results = pl.pallas_call(
        functools.partial(kernel, n, local_len, own),
        out_shape=(
            jax.ShapeDtypeStruct((channels, local_len), jnp.bfloat16),
            jax.ShapeDtypeStruct((3, channels, local_len), jnp.bfloat16),
            jax.ShapeDtypeStruct((3, TAPS, channels), F32),
            jax.ShapeDtypeStruct((own, MODES), F32),
            jax.ShapeDtypeStruct((own, MODES), F32),
            jax.ShapeDtypeStruct((1, own), F32),
        ),
        in_specs=[anywhere, anywhere, vmem, vmem, vmem, vmem],
        out_specs=(anywhere, anywhere, vmem, vmem, vmem, vmem),
        scratch_shapes=[
            pltpu.VMEM((n, 4, own, local_len), jnp.bfloat16),
            pltpu.VMEM((4, tiles, OFF + local_len, 128), F32),
            stepped,
            stepped,
            stepped,
            stepped,
            stepped,
            stepped,
            stepped,
            pltpu.VMEM((3, tiles, local_len + 8, 128), F32),
            pltpu.VMEM((1, tiles, local_len, 128), F32),
            pltpu.VMEM((n, 4, own, local_len), jnp.bfloat16),
            pltpu.VMEM((16, 128), F32),
            pltpu.VMEM((n, 16, 128), F32),
            pltpu.VMEM((4, 128, 128), F32),
            pltpu.VMEM((10, SUB, 128), F32),
            pltpu.VMEM((MODES, SUB, 128), F32),
            pltpu.VMEM((MODES, SUB, 128), F32),
            pltpu.VMEM((2, tiles, MODES, 128), F32),
            pltpu.VMEM((2, tiles, MODES, SUB, 128), F32),
            pltpu.VMEM((MODES, SUB, 128), F32),
            pltpu.VMEM((MODES, SUB, 128), F32),
            pltpu.SemaphoreType.DMA((5,)),
            pltpu.SemaphoreType.DMA((5,)),
            pltpu.SemaphoreType.DMA((2,)),
        ],
        compiler_params=pltpu.CompilerParams(
            collective_id=0, has_side_effects=True, vmem_limit_bytes=32 * 1024 * 1024
        ),
    )(
        projected,
        cotangent,
        short_weight.transpose(0, 2, 1),
        decay_rates,
        residues,
        skip_weight.reshape(1, -1),
    )
    output, grad_projected, grad_short, grad_res, grad_dec, grad_skip = results
    return (
        output,
        grad_projected,
        grad_short.transpose(0, 2, 1),
        grad_res,
        grad_dec,
        grad_skip.reshape(-1),
    )


def solution(mesh):
    return jax.shard_map(
        per_device,
        mesh=mesh,
        in_specs=(
            P(None, "tensor", "context"),
            P(None, "tensor", None),
            P(("tensor", "context"), None),
            P(("tensor", "context"), None),
            P(("tensor", "context")),
            P("tensor", "context"),
        ),
        out_specs=(
            P("tensor", "context"),
            P(None, "tensor", "context"),
            P(None, "tensor", None),
            P(("tensor", "context"), None),
            P(("tensor", "context"), None),
            P(("tensor", "context")),
        ),
        check_vma=False,
    )
```

time: 254 us -> 56.4 us (0.22); the launches traced: 249 us -> 56 us
  blocking collectives: 129 us -> 0 us
  Pallas kernels: 0 us -> 47 us
  matrix products: 31.6 us -> 0 us
  starting transfers between devices: 29.8 us -> 0 us
  other arithmetic: 20 us -> 0 us
  waiting for transfers between devices: 17.6 us -> 0 us
  local copies, waits for them, and re-layouts: 18.7 us -> 8.39 us
    psum x1 -> x0, blocking collectives: 129 us -> none  [per_device(): grad_short = lax.psum(partial_taps, 'context') / math.sqrt(length)]
    pallas_call x0 -> x1, Pallas kernels: none -> 47 us  [per_device(): pl.pallas_call(functools.partial(kernel, n, local_len, own), out_shape=(j...]
    dot_general x36 -> x0, matrix products: 31.6 us -> none  [the longest x24 19.7 us: inner_product(): return jnp.einsum('ckb,bm->ckm', left, table, precision=PRECISE)]
    all_to_all x4 -> x0, starting transfers between devices: 22.5 us -> none  [the longest x1 8.15 us: per_device(): lax.all_to_all(gated_signal, 'context', split_axis=0, concat_axis=1, tile...]
    all_to_all x4 -> x0, waiting for transfers between devices: 15.4 us -> none  [the longest x1 5.76 us: per_device(): lax.all_to_all(gated_signal, 'context', split_axis=0, concat_axis=1, tile...]
    div x6 -> x0, local copies, waits for them, and re-layouts: 9.41 us -> none  [inverse_dft(): return blocks.reshape(channels, -1) / total]
    reduce_sum x18 -> x0, other arithmetic: 9.4 us -> none  [the longest x16 4.16 us: one_mode(): plain = jnp.sum(grad_filter * weights, axis=1)]
    ppermute x2 -> x0, starting transfers between devices: 7.24 us -> none  [passed_along(): return lax.ppermute(block, axis, route)]
  transfers between devices with their start and end apart: 6 -> 0, of which waited for: 5 -> 0; matrix products, arithmetic and copies ran while one was open for 11% -> 0% of each run, Pallas kernels for 0% -> 0%
where the time goes in v1:
time: 56.4 us; the launch traced here: 56 us
  Pallas kernels  47 us (83%)
  local copies, waits for them, and re-layouts  8.39 us (15%)
  between operations  0.66 us (1%)
    pallas_call x1, Pallas kernels, per_device(): pl.pallas_call(functools.partial(kernel, n, local_len, own), out_shape=(j...  47 us
    unnamed x18, local copies, waits for them, and re-layouts  8.39 us

profile of v1, /device:TPU:1, one launch (start us, length us, event | category | flops | bytes accessed | tf_op | source)
XLA Modules:
  0.0 56.0 jit_solution(2291690013724937495)
XLA Ops:
  0.6 0.0 copy-start.5
  0.6 0.6 %copy-done.5 = f32[16]{0:T(128)S(1)} copy-done((f32[16]{0:T(128)S(1)}, f32[16]{0:T(128)}, u32[]{:S(2)}) %copy-start.5) | copy-done | bytes 88
  1.3 0.0 copy-start
  1.3 1.0 %copy-done = bf16[3,512,128]{2,1,0:T(8,128)(2,1)S(1)} copy-done((bf16[3,512,128]{2,1,0:T(8,128)(2,1)S(1)}, bf16[3,512,128]{2,1,0:T(8,128)(2,1)}, u32[]{:S(2)}) %copy-start) | copy-done | bytes 393240
  2.3 0.0 copy-start.1
  2.3 0.9 %copy-done.1 = bf16[512,128]{1,0:T(8,128)(2,1)S(1)} copy-done((bf16[512,128]{1,0:T(8,128)(2,1)S(1)}, bf16[512,128]{1,0:T(8,128)(2,1)}, u32[]{:S(2)}) %copy-start.1) | copy-done | bytes 131096
  3.2 0.0 copy-start.2
  3.2 0.7 %copy-done.2 = f32[3,512,3]{1,2,0:T(4,128)S(1)} copy-done((f32[3,512,3]{1,2,0:T(4,128)S(1)}, f32[3,512,3]{1,2,0:T(4,128)}, u32[]{:S(2)}) %copy-start.2) | copy-done | bytes 18456
  3.9 0.0 copy-start.3
  3.9 0.7 %copy-done.3 = f32[16,16]{1,0:T(8,128)S(1)} copy-done((f32[16,16]{1,0:T(8,128)S(1)}, f32[16,16]{1,0:T(8,128)}, u32[]{:S(2)}) %copy-start.3) | copy-done | bytes 1048
  4.6 0.0 copy-start.4
  4.6 0.7 %copy-done.4 = f32[16,16]{1,0:T(8,128)S(1)} copy-done((f32[16,16]{1,0:T(8,128)S(1)}, f32[16,16]{1,0:T(8,128)}, u32[]{:S(2)}) %copy-start.4) | copy-done | bytes 1048
  5.3 47.0 %shard_map.109 = (bf16[512,128]{1,0:T(8,128)(2,1)S(1)}, bf16[3,512,128]{2,1,0:T(8,128)(2,1)S(1)}, f32[3,3,512]{2,1,0:T(4,128)S(1)}, f32[16,16]{1,0:T(8,128)S(1)}...) custom-call(bf16[3,512,128]{2,1,0:T(8,128)(2,1)S(1)} %copy-done, bf16[512,128]{1,0:T(8,128)(2,1)S(1)} %copy-done.1, ...), custom_call_target="tpu_custom_call" | custom-call | tf_op jit(solution)/shard_map/pallas_call | solution.py:469
  52.3 0.7 %copy.18 = bf16[512,128]{1,0:T(8,128)(2,1)} copy(bf16[512,128]{1,0:T(8,128)(2,1)S(1)} %get-tuple-element.24) | data formatting | bytes 262144
  53.0 0.7 %copy.19 = bf16[3,512,128]{2,1,0:T(8,128)(2,1)} copy(bf16[3,512,128]{2,1,0:T(8,128)(2,1)S(1)} %get-tuple-element.25) | data formatting | bytes 786432
  53.7 0.6 %copy.20 = f32[3,512,3]{1,2,0:T(4,128)} copy(f32[3,512,3]{1,2,0:T(4,128)S(1)} %bitcast.5) | data formatting | bytes 36864
  54.3 0.6 %copy.21 = f32[16,16]{1,0:T(8,128)} copy(f32[16,16]{1,0:T(8,128)S(1)} %get-tuple-element.27) | data formatting | bytes 2048
  54.9 0.6 %copy.22 = f32[16,16]{1,0:T(8,128)} copy(f32[16,16]{1,0:T(8,128)S(1)} %get-tuple-element.28) | data formatting | bytes 2048
  55.5 0.5 copy.23
Async XLA Ops:
  0.6 0.7 %copy-start.5 = (f32[16]{0:T(128)S(1)}, f32[16]{0:T(128)}, u32[]{:S(2)}) copy-start(f32[16]{0:T(128)} %param.10) | copy-start | bytes 196
  1.3 1.0 %copy-start = (bf16[3,512,128]{2,1,0:T(8,128)(2,1)S(1)}, bf16[3,512,128]{2,1,0:T(8,128)(2,1)}, u32[]{:S(2)}) copy-start(bf16[3,512,128]{2,1,0:T(8,128)(2,1)} %proj_ref.1) | copy-start | bytes 1179652
  2.3 0.9 %copy-start.1 = (bf16[512,128]{1,0:T(8,128)(2,1)S(1)}, bf16[512,128]{1,0:T(8,128)(2,1)}, u32[]{:S(2)}) copy-start(bf16[512,128]{1,0:T(8,128)(2,1)} %cot_ref.1) | copy-start | bytes 393220
  3.2 0.7 %copy-start.2 = (f32[3,512,3]{1,2,0:T(4,128)S(1)}, f32[3,512,3]{1,2,0:T(4,128)}, u32[]{:S(2)}) copy-start(f32[3,512,3]{1,2,0:T(4,128)} %param.7) | copy-start | bytes 55300
  3.9 0.7 %copy-start.3 = (f32[16,16]{1,0:T(8,128)S(1)}, f32[16,16]{1,0:T(8,128)}, u32[]{:S(2)}) copy-start(f32[16,16]{1,0:T(8,128)} %decay_ref.1) | copy-start | bytes 3076
  4.6 0.7 %copy-start.4 = (f32[16,16]{1,0:T(8,128)S(1)}, f32[16,16]{1,0:T(8,128)}, u32[]{:S(2)}) copy-start(f32[16,16]{1,0:T(8,128)} %res_ref.1) | copy-start | bytes 3076

commit v2 on v0

v2 whole, which is shorter than its diff:
```python
import functools
import math

import jax
import jax.numpy as jnp
from jax import lax
from jax.experimental import pallas as pl
from jax.experimental.pallas import tpu as pltpu
from jax.sharding import PartitionSpec as P

MESH = pl.DeviceIdType.MESH
SUB = 8
MODES = 16
TAPS = 3
OFF = 8
RUNS = 4
WIDE = 4
HALF = RUNS * WIDE
F32 = jnp.float32
BF16 = jnp.bfloat16


def rounded(value):
    return value.astype(BF16).astype(F32)


def one_minus_exp(x):
    series = jnp.ones_like(x)
    for k in range(10, 1, -1):
        series = 1.0 - x * (1.0 / k) * series
    return jnp.where(x < 0.5, x * series, 1.0 - jnp.exp(-x))


def kernel(
    n,
    local_len,
    own,
    proj_ref,
    cot_ref,
    sw_hbm,
    decay_hbm,
    res_hbm,
    skip_hbm,
    out_ref,
    gproj_ref,
    gshort_ref,
    gres_ref,
    gdec_ref,
    gskip_ref,
    rx,
    so,
    xt,
    qs,
    ks,
    vs,
    us,
    gs,
    cv,
    gf,
    ot,
    sw,
    filt,
    par,
    wt,
    lam,
    coef,
    tots,
    ins,
    ends,
    edge,
    edge_in,
    sums,
    sums_in,
    shorts,
    all_short,
    pacc,
    racc,
    send_sem,
    recv_sem,
    local_sem,
):
    me = lax.axis_index("context")
    length = n * local_len
    steps = local_len // SUB
    chans = 2 * own
    root = math.sqrt(length)
    run_len = WIDE * local_len
    side = lax.rem(me // WIDE, 2)
    my_x = me // (2 * WIDE)
    my_w = lax.rem(me, WIDE)
    my_slot = my_x * WIDE + my_w
    partner = me + WIDE * (1 - 2 * side)
    is_a = side == 0

    def each_peer(body):
        def step(t, carry):
            slot = lax.rem(my_slot + t, HALF)
            x, w = slot // WIDE, lax.rem(slot, WIDE)
            body(slot, x, w, (2 * x + side) * WIDE + w)
            return carry

        lax.fori_loop(1, HALF, step, 0)

    def remote(src, dst, k, device):
        return pltpu.make_async_remote_copy(
            src_ref=src,
            dst_ref=dst,
            send_sem=send_sem.at[k],
            recv_sem=recv_sem.at[k],
            device_id={"context": device},
            device_id_type=MESH,
        )

    def arrived(ref, k):
        pltpu.make_async_copy(ref, ref, recv_sem.at[k]).wait()

    def left(ref, k):
        pltpu.make_async_copy(ref, ref, send_sem.at[k]).wait()

    barrier = pltpu.get_barrier_semaphore()
    pl.semaphore_signal(barrier, inc=1, device_id={"context": partner}, device_id_type=MESH)
    each_peer(
        lambda slot, x, w, device: pl.semaphore_signal(
            barrier, inc=1, device_id={"context": device}, device_id_type=MESH
        )
    )
    small = [
        pltpu.make_async_copy(sw_hbm, sw, local_sem.at[0]),
        pltpu.make_async_copy(decay_hbm, filt.at[0], local_sem.at[1]),
        pltpu.make_async_copy(res_hbm, filt.at[1], local_sem.at[2]),
        pltpu.make_async_copy(skip_hbm, filt.at[2, pl.ds(0, 1)], local_sem.at[3]),
    ]
    keep = [
        pltpu.make_async_copy(
            proj_ref.at[:, my_x, :, my_w], rx.at[my_slot, pl.ds(0, 3)], local_sem.at[4]
        ),
        pltpu.make_async_copy(cot_ref.at[my_x, :, my_w], rx.at[my_slot, 3], local_sem.at[5]),
    ]
    for copy in small + keep:
        copy.start()

    lane = lax.broadcasted_iota(jnp.int32, (1, 128), 1)
    group = lane // chans
    sub_row = lax.broadcasted_iota(jnp.int32, (SUB, 128), 0)
    corner = jnp.logical_and(sub_row == 0, group == 0)

    def group_sum(rows):
        width = chans
        while width < 128:
            rows = rows + pltpu.roll(rows, width, 1)
            width *= 2
        return rows

    def to_group(rows, here, there):
        shift = ((there - here) * chans) % 128
        return pltpu.roll(rows, shift, 1) if shift else rows

    def packed(tiles, here):
        total = None
        for jt in range(RUNS):
            piece = jnp.where(group == jt, to_group(tiles[jt], here, jt), 0.0)
            total = piece if total is None else total + piece
        return total

    def repeated(rows, jt):
        return group_sum(jnp.where(group == jt, rows, 0.0))

    def before(rows):
        return jnp.where(group >= 1, pltpu.roll(rows, chans, 1), 0.0)

    def after(rows):
        return jnp.where(group < RUNS - 1, pltpu.roll(rows, 128 - chans, 1), 0.0)

    for copy in small:
        copy.wait()
    pl.semaphore_wait(barrier, HALF)

    remote(filt.at[pl.ds(0, 3)], filt.at[pl.ds(3, 3)], 3, partner).start()

    def send_kv(slot, x, w, device):
        remote(proj_ref.at[pl.ds(1, 2), x, :, w], rx.at[my_slot, pl.ds(1, 2)], 0, device).start()

    def send_q_cot(slot, x, w, device):
        remote(proj_ref.at[0, x, :, w], rx.at[my_slot, 0], 1, device).start()
        remote(cot_ref.at[x, :, w], rx.at[my_slot, 3], 2, device).start()

    each_peer(send_kv)
    each_peer(send_q_cot)

    for i in range(3):
        rows = jnp.concatenate(
            [
                sw[i, :, pl.ds(pl.multiple_of(my_x * 128, 128), 128)],
                jnp.zeros((SUB - TAPS, 128), F32),
            ],
            axis=0,
        )
        rows = pltpu.roll(rows, lax.rem(128 - my_w * own, 128), 1)
        rows = jnp.where(lane < own, rows, 0.0) + pltpu.roll(
            jnp.where(jnp.logical_and(lane >= 64, lane < 64 + own), rows, 0.0), 64 + own, 1
        )
        rows = group_sum(rows)
        for j in range(TAPS):
            wt[TAPS * i + j] = jnp.broadcast_to(rows[j : j + 1, :], (SUB, 128))
    for copy in keep:
        copy.wait()
    arrived(filt.at[pl.ds(3, 3)], 3)
    par[...] = jnp.zeros_like(par)
    for k in range(2):
        mine, theirs = filt[k], filt[3 + k]
        first, second = jnp.where(is_a, mine, theirs), jnp.where(is_a, theirs, mine)
        for g in range(128 // chans):
            par[k, g * chans : g * chans + own, 0:MODES] = first
            par[k, g * chans + own : (g + 1) * chans, 0:MODES] = second
    mine, theirs = filt[2, 0:1, :], filt[5, 0:1, :]
    par[2, 0:1, 0:own] = jnp.where(is_a, mine, theirs)
    par[2, 1:2, 0:own] = jnp.where(is_a, theirs, mine)
    skip_row = group_sum(par[2, 0:1, :] + pltpu.roll(par[2, 1:2, :], own, 1))
    wt[9] = jnp.broadcast_to(skip_row, (SUB, 128))
    per = par[0].T[0:MODES, :] * (1.0 / length)
    residue = par[1].T[0:MODES, :]
    scale = jnp.sqrt(one_minus_exp(2.0 * per))
    coef_rows = residue * scale
    lam_rows = jnp.exp(-per)
    inv_lam = jnp.exp(per)
    par[3, 0:MODES, :] = per
    for m in range(MODES):
        lam[m] = jnp.broadcast_to(lam_rows[m : m + 1, :], (SUB, 128))
        coef[m] = jnp.broadcast_to(coef_rows[m : m + 1, :], (SUB, 128))

    def power(span):
        return jnp.exp(per * (-1.0 * span))

    sub_spans = [1, 2, 4]
    run_span, pair_span = power(run_len), power(2 * run_len)
    up_span = jnp.exp(per * (-1.0 * local_len) * group.astype(F32))
    down_span = jnp.exp(per * (-1.0 * local_len) * (WIDE - 1 - group).astype(F32))

    def turn(arrays):
        def tile(jt, carry):
            for a in arrays:
                block = rx[pl.ds(WIDE * jt, WIDE), a].reshape(128, local_len).astype(F32)
                turned = block.T
                xt[a, jt, OFF : OFF + local_len, :] = turned
                if a < 3:
                    xt[a, jt, 0:OFF, :] = jnp.where(
                        group == 0, 0.0, pltpu.roll(turned[local_len - OFF :, :], chans, 1)
                    )
            return carry

        lax.fori_loop(0, RUNS, tile, 0)

    def path(a, jt, p):
        total = None
        for j in range(TAPS):
            term = wt[TAPS * a + j] * xt[a, jt, pl.ds(OFF + p - j, SUB, stride=steps), :]
            total = term if total is None else total + term
        return total

    def last_rows(a):
        return packed(
            [xt[a, jt, OFF + local_len - 8 : OFF + local_len, :] for jt in range(RUNS)], WIDE - 1
        )[6:8, :]

    def first_rows(a):
        return packed([xt[a, jt, OFF : OFF + 8, :] for jt in range(RUNS)], 0)[0:2, :]

    def edge_path(a, first, last):
        w = [wt[TAPS * a + j][0:1, :] for j in range(TAPS)]
        return (
            w[0] * first[0:1] + w[1] * last[1:2] + w[2] * last[0:1],
            w[0] * first[1:2] + w[1] * first[0:1] + w[2] * last[1:2],
        )

    def mine_before(rows):
        return jnp.where(is_a, rows, before(rows))

    def theirs_before(rows):
        return jnp.where(is_a, before(rows), rows)

    def theirs_after(rows):
        return jnp.where(is_a, rows, after(rows))

    def fill_rim(a, rows):
        for jt in range(RUNS):
            rim = to_group(rows, jt, 0)
            xt[a, jt, OFF - 2 : OFF, :] = jnp.where(group == 0, rim, xt[a, jt, OFF - 2 : OFF, :])

    many = 8

    def block_ends(k, signal, reverse):
        def some(at, carry):
            jt = at // (MODES // many)
            first = lax.rem(at, MODES // many) * many
            lams = [lam[first + i] for i in range(many)]
            state = [None] * many
            for p in reversed(range(steps)) if reverse else range(steps):
                x = signal[jt, p]
                for i in range(many):
                    state[i] = x if state[i] is None else lams[i] * state[i] + x
            for i in range(many):
                pers = jnp.broadcast_to(par[3, pl.ds(first + i, 1), :], (SUB, 128))
                s = state[i]
                for d in sub_spans:
                    factor = jnp.exp(pers * (-1.0 * steps * d))
                    if reverse:
                        moved = jnp.where(sub_row < SUB - d, pltpu.roll(s, SUB - d, 0), 0.0)
                    else:
                        moved = jnp.where(sub_row >= d, pltpu.roll(s, d, 0), 0.0)
                    s = s + factor * moved
                if reverse:
                    ins[k, jt, first + i] = jnp.where(
                        sub_row < SUB - 1, pltpu.roll(s, SUB - 1, 0), 0.0
                    )
                    tots[k, jt, pl.ds(first + i, 1), :] = s[0:1, :]
                else:
                    ins[k, jt, first + i] = jnp.where(sub_row >= 1, pltpu.roll(s, 1, 0), 0.0)
                    tots[k, jt, pl.ds(first + i, 1), :] = s[SUB - 1 : SUB, :]
            return carry

        lax.fori_loop(0, RUNS * (MODES // many), some, 0)

    def run_ends(k, reverse):
        tiles = []
        for jt in range(RUNS):
            s = tots[k, jt]
            for d in (1, 2):
                if reverse:
                    moved = jnp.where(group < WIDE - d, pltpu.roll(s, 128 - chans * d, 1), 0.0)
                else:
                    moved = jnp.where(group >= d, pltpu.roll(s, chans * d, 1), 0.0)
                s = s + power(local_len * d) * moved
            tiles.append(s)
            tots[k, jt] = after(s) if reverse else before(s)
        return packed(tiles, 0 if reverse else WIDE - 1)

    arrived(rx.at[pl.ds(0, HALF - 1), pl.ds(1, 2)], 0)
    turn((1, 2))

    def gate_kv(jt, carry):
        for p in range(steps):
            key, value = path(1, jt, p), path(2, jt, p)
            u = rounded(key * value)
            ks[jt, p] = key
            vs[jt, p] = value
            us[jt, p] = jnp.where(corner, 0.0, u) if p < 2 else u
        return carry

    lax.fori_loop(0, RUNS, gate_kv, 0)
    block_ends(0, us, False)
    my_f = run_ends(0, False)
    k_last, v_last = last_rows(1), last_rows(2)
    k_first, v_first = first_rows(1), first_rows(2)
    edge[0, 0:MODES, :] = my_f
    edge[0, MODES : MODES + 8, :] = jnp.concatenate([k_last, v_last, k_first, v_first], axis=0)
    remote(edge.at[0], edge_in.at[0], 4, partner).start()

    arrived(rx.at[pl.ds(0, HALF - 1), 0], 1)
    arrived(rx.at[pl.ds(0, HALF - 1), 3], 2)
    turn((0, 3))

    def gate_q(jt, carry):
        for p in range(steps):
            query = path(0, jt, p)
            g = rounded(xt[3, jt, pl.ds(OFF + p, SUB, stride=steps), :] * query)
            qs[jt, p] = query
            gs[jt, p] = jnp.where(corner, 0.0, g) if p < 2 else g
        return carry

    lax.fori_loop(0, RUNS, gate_q, 0)
    block_ends(1, gs, True)
    my_b = run_ends(1, True)
    q_last, q_first, c_first = last_rows(0), first_rows(0), first_rows(3)
    edge[1, 0:MODES, :] = my_b
    edge[1, MODES : MODES + 8, :] = jnp.concatenate(
        [q_last, q_first, c_first, jnp.zeros((2, 128), F32)], axis=0
    )
    remote(edge.at[1], edge_in.at[1], 5, partner).start()

    arrived(edge_in.at[0], 4)
    their_f = edge_in[0, 0:MODES, :]
    rows = edge_in[0, MODES : MODES + 8, :]
    tk_last, tv_last, tk_first, tv_first = rows[0:2], rows[2:4], rows[4:6], rows[6:8]
    fill_rim(1, theirs_before(tk_last))
    fill_rim(2, theirs_before(tv_last))

    def regate_kv(jt, carry):
        for p in range(2):
            key, value = path(1, jt, p), path(2, jt, p)
            ks[jt, p] = key
            vs[jt, p] = value
            us[jt, p] = rounded(key * value)
        return carry

    lax.fori_loop(0, RUNS, regate_kv, 0)
    my_k = edge_path(1, k_first, theirs_before(tk_last))
    my_v = edge_path(2, v_first, theirs_before(tv_last))
    their_k = edge_path(1, tk_first, mine_before(k_last))
    their_v = edge_path(2, tv_first, mine_before(v_last))
    my_u = [rounded(k * v) for k, v in zip(my_k, my_v)]
    their_u = [rounded(k * v) for k, v in zip(their_k, their_v)]
    late = (power(run_len - 1), power(run_len - 2))
    my_f = my_f + late[0] * my_u[0] + late[1] * my_u[1]
    their_f = their_f + late[0] * their_u[0] + late[1] * their_u[1]
    a_f, b_f = jnp.where(is_a, my_f, their_f), jnp.where(is_a, their_f, my_f)
    scan = run_span * a_f + b_f
    scan = scan + pair_span * before(scan)
    scan = scan + power(4 * run_len) * jnp.where(group >= 2, pltpu.roll(scan, 2 * chans, 1), 0.0)
    into_a = before(scan)
    carry_f = jnp.where(is_a, into_a, run_span * into_a + a_f)
    next_f = run_span * carry_f + my_f
    whole_f = carry_f + inv_lam * (my_u[0] + inv_lam * my_u[1])
    for jt in range(RUNS):
        tots[0, jt] = tots[0, jt] + up_span * repeated(whole_f, jt)
        ends[jt] = repeated(carry_f, jt)

    def in_state(k, jt, m):
        pers = jnp.broadcast_to(par[3, pl.ds(m, 1), :], (SUB, 128))
        into = jnp.broadcast_to(tots[k, jt, pl.ds(m, 1), :], (SUB, 128))
        away = (sub_row if k == 0 else SUB - 1 - sub_row).astype(F32)
        state = ins[k, jt, m] + jnp.exp(pers * (-1.0 * steps) * away) * into
        if k == 0:
            exact = jnp.broadcast_to(ends[jt, pl.ds(m, 1), :], (SUB, 128))
            state = jnp.where(corner, exact, state)
        return state

    def filtered_by_modes(k, signal, jt):
        def some(at, totals):
            totals = list(totals)
            first = at * many
            lams = [lam[first + i] for i in range(many)]
            coefs = [coef[first + i] for i in range(many)]
            state = [in_state(k, jt, first + i) for i in range(many)]
            for i in range(many):
                ins[k, jt, first + i] = state[i]
            for p in reversed(range(steps)) if k else range(steps):
                x = signal[jt, p]
                parts = []
                for i in range(many):
                    state[i] = lams[i] * state[i] + x
                    parts.append(coefs[i] * state[i])
                while len(parts) > 1:
                    parts = [parts[i] + parts[i + 1] for i in range(0, len(parts), 2)]
                totals[p] = totals[p] + parts[0]
            return tuple(totals)

        skip = wt[9]
        start = tuple(skip * signal[jt, p] for p in range(steps))
        return lax.fori_loop(0, MODES // many, some, start)

    def conv_tile(jt, carry):
        totals = filtered_by_modes(0, us, jt)
        for p in range(steps):
            cv[jt, p] = rounded(totals[p])
        return carry

    lax.fori_loop(0, RUNS, conv_tile, 0)

    arrived(edge_in.at[1], 5)
    their_b = edge_in[1, 0:MODES, :]
    rows = edge_in[1, MODES : MODES + 8, :]
    tq_last, tq_first, tc_first = rows[0:2], rows[2:4], rows[4:6]
    fill_rim(0, theirs_before(tq_last))

    def regate_q(jt, carry):
        for p in range(2):
            query = path(0, jt, p)
            qs[jt, p] = query
            gs[jt, p] = rounded(xt[3, jt, pl.ds(OFF + p, SUB, stride=steps), :] * query)
        return carry

    lax.fori_loop(0, RUNS, regate_q, 0)

    def output_tile(jt, carry):
        for p in range(steps):
            at = pl.ds(p, SUB, stride=steps)
            conv = cv[jt, p]
            ot[jt, at, :] = qs[jt, p] * conv
            gf[0, jt, at, :] = xt[3, jt, pl.ds(OFF + p, SUB, stride=steps), :] * conv
        so[pl.ds(WIDE * jt, WIDE), 0] = (
            ot[jt].T.astype(BF16).reshape(WIDE, 2, own, local_len)
        )
        return carry

    lax.fori_loop(0, RUNS, output_tile, 0)

    def send_out(slot, x, w, device):
        remote(so.at[slot, 0], out_ref.at[my_x, :, my_w], 6, device).start()

    each_peer(send_out)

    my_q = edge_path(0, q_first, theirs_before(tq_last))
    their_q = edge_path(0, tq_first, mine_before(q_last))
    my_g = [rounded(my_q[i] * c_first[i : i + 1]) for i in range(2)]
    their_g = [rounded(their_q[i] * tc_first[i : i + 1]) for i in range(2)]
    my_b = my_b + my_g[0] + lam_rows * my_g[1]
    their_b = their_b + their_g[0] + lam_rows * their_g[1]
    a_b, b_b = jnp.where(is_a, my_b, their_b), jnp.where(is_a, their_b, my_b)
    scan = a_b + run_span * b_b
    scan = scan + pair_span * after(scan)
    scan = scan + power(4 * run_len) * jnp.where(
        group < RUNS - 2, pltpu.roll(scan, 128 - 2 * chans, 1), 0.0
    )
    into_b = after(scan)
    carry_b = jnp.where(is_a, run_span * into_b + b_b, into_b)
    for jt in range(RUNS):
        tots[1, jt] = tots[1, jt] + down_span * repeated(carry_b, jt)

    next_u = [theirs_after(u) for u in their_u]
    next_g = [theirs_after(g) for g in their_g]
    state0 = lam_rows * next_f + next_u[0]
    state1 = lam_rows * state0 + next_u[1]
    back0 = carry_b
    back1 = inv_lam * (carry_b - next_g[0])
    beyond = [[], [], []]
    for i, (state, back) in enumerate(((state0, back0), (state1, back1))):
        conv = rounded(
            jnp.sum(coef_rows * state, axis=0, keepdims=True) + skip_row * next_u[i]
        )
        back = rounded(jnp.sum(coef_rows * back, axis=0, keepdims=True) + skip_row * next_g[i])
        beyond[0].append(theirs_after(tc_first[i : i + 1]) * conv)
        beyond[1].append(back * theirs_after(their_v[i]))
        beyond[2].append(back * theirs_after(their_k[i]))

    def gf_rim(a):
        rows = jnp.concatenate(beyond[a] + [jnp.zeros((6, 128), F32)], axis=0)
        for jt in range(RUNS):
            inner = pltpu.roll(gf[a, jt, 0:8, :], 128 - chans, 1)
            gf[a, jt, local_len : local_len + 8, :] = jnp.where(
                group == WIDE - 1, to_group(rows, jt, WIDE - 1), inner
            )

    def grad_path(a, jt):
        total = None
        for j in range(TAPS):
            w = jnp.broadcast_to(wt[TAPS * a + j][0:1, :], (local_len, 128))
            term = w * gf[a, jt, j : j + local_len, :]
            total = term if total is None else total + term
        so[pl.ds(WIDE * jt, WIDE), 1 + a] = (
            total.T.astype(BF16).reshape(WIDE, 2, own, local_len)
        )

    def grad_taps(a, jt):
        return [
            jnp.sum(
                gf[a, jt, 0:local_len, :] * xt[a, jt, OFF - j : OFF - j + local_len, :],
                axis=0,
                keepdims=True,
            )
            for j in range(TAPS)
        ]

    gf_rim(0)

    def grad_q_tile(jt, carry):
        grad_path(0, jt)
        return carry

    lax.fori_loop(0, RUNS, grad_q_tile, 0)

    def send_gq(slot, x, w, device):
        remote(so.at[slot, 1], gproj_ref.at[0, my_x, :, my_w], 7, device).start()

    each_peer(send_gq)

    def back_tile(jt, skip_total):
        totals = filtered_by_modes(1, gs, jt)
        for p in range(steps):
            at = pl.ds(p, SUB, stride=steps)
            back = rounded(totals[p])
            gf[1, jt, at, :] = back * vs[jt, p]
            gf[2, jt, at, :] = back * ks[jt, p]
            skip_total = skip_total + us[jt, p] * gs[jt, p]
        return skip_total

    skip_total = lax.fori_loop(0, RUNS, back_tile, jnp.zeros((SUB, 128), F32))
    gf_rim(1)
    gf_rim(2)

    def grad_kv_tile(jt, carry):
        grad_path(1, jt)
        grad_path(2, jt)
        return carry

    lax.fori_loop(0, RUNS, grad_kv_tile, 0)

    def send_gkv(slot, x, w, device):
        remote(
            so.at[slot, pl.ds(2, 2)], gproj_ref.at[pl.ds(1, 2), my_x, :, my_w], 8, device
        ).start()

    each_peer(send_gkv)
    keep_out = [
        pltpu.make_async_copy(so.at[my_slot, 0], out_ref.at[my_x, :, my_w], local_sem.at[0]),
        pltpu.make_async_copy(
            so.at[my_slot, pl.ds(1, 3)], gproj_ref.at[:, my_x, :, my_w], local_sem.at[1]
        ),
    ]
    for copy in keep_out:
        copy.start()

    def taps_tile(jt, carry):
        found = [part for a in range(3) for part in grad_taps(a, jt)]
        return tuple(c + f for c, f in zip(carry, found))

    found = lax.fori_loop(0, RUNS, taps_tile, tuple(jnp.zeros((1, 128), F32) for _ in range(9)))
    rows = jnp.concatenate(
        list(found)
        + [jnp.sum(skip_total, axis=0, keepdims=True), jnp.zeros((6, 128), F32)],
        axis=0,
    )
    my_short = group_sum(rows) * (1.0 / root)
    sums[0, 0:16, :] = my_short
    remote(sums.at[0, pl.ds(0, 16)], sums_in.at[0, pl.ds(0, 16)], 9, partner).start()

    pacc[...] = jnp.zeros_like(pacc)
    racc[...] = jnp.zeros_like(racc)
    pair = 2

    def mode_sums(at, carry):
        jt = at // (MODES // pair)
        first = lax.rem(at, MODES // pair) * pair
        lams = [lam[first + i] for i in range(pair)]
        behind = [[None] * steps + [ins[1, jt, first + i]] for i in range(pair)]
        for p in reversed(range(1, steps)):
            g = gs[jt, p]
            for i in range(pair):
                behind[i][p] = lams[i] * behind[i][p + 1] + g
        plain = [None] * pair
        ramped = [None] * pair
        state = [ins[0, jt, first + i] for i in range(pair)]
        for p in range(steps):
            u = us[jt, p]
            g = gs[jt, p]
            for i in range(pair):
                state[i] = lams[i] * state[i] + u
                flat = g * state[i]
                ramp = behind[i][p + 1] * state[i]
                plain[i] = flat if plain[i] is None else plain[i] + flat
                ramped[i] = ramp if ramped[i] is None else ramped[i] + ramp
        for i in range(pair):
            pacc[first + i] += plain[i]
            racc[first + i] += ramped[i]
        return carry

    lax.fori_loop(0, RUNS * (MODES // pair), mode_sums, 0)
    my_plain = group_sum(
        jnp.concatenate([jnp.sum(pacc[m], axis=0, keepdims=True) for m in range(MODES)], axis=0)
    )
    my_ramped = group_sum(
        jnp.concatenate([jnp.sum(racc[m], axis=0, keepdims=True) for m in range(MODES)], axis=0)
    )
    sums[1, 0:MODES, :] = my_plain
    sums[1, MODES : 2 * MODES, :] = my_ramped
    remote(sums.at[1], sums_in.at[1], 10, partner).start()

    arrived(sums_in.at[0, pl.ds(0, 16)], 9)
    short = my_short + sums_in[0, 0:16, :]
    odd = lax.rem(my_w, 2) == 1
    other = pltpu.roll(short, own, 1)
    low, high = jnp.where(odd, other, short), jnp.where(odd, short, other)
    place = lane // own
    shorts[...] = jnp.where(place == my_w, low, jnp.where(place == my_w + WIDE, high, 0.0))
    each_peer(
        lambda slot, x, w, device: remote(shorts, all_short.at[my_slot], 11, device).start()
    )
    all_short[my_slot] = shorts[...]
    gskip_ref[...] = jnp.where(is_a, short[9:10, 0:own], short[9:10, own : 2 * own])

    arrived(sums_in.at[1], 10)
    plain = my_plain + sums_in[1, 0:MODES, :]
    ramped = lam_rows * (my_ramped + sums_in[1, MODES : 2 * MODES, :])
    grad_res = scale * plain / root
    grad_dec = residue * (jnp.exp(-2.0 * per) / scale * plain - scale * ramped) / (length * root)
    par[0, 0:MODES, :] = grad_res
    par[1, 0:MODES, :] = grad_dec
    for k, ref in ((0, gres_ref), (1, gdec_ref)):
        turned = par[k].T
        ref[...] = jnp.where(is_a, turned[0:own, 0:MODES], turned[own : 2 * own, 0:MODES])

    arrived(all_short.at[pl.ds(0, HALF - 1)], 11)
    for jt in range(RUNS):
        total = all_short[WIDE * jt]
        for w in range(1, WIDE):
            total = total + all_short[WIDE * jt + w]
        for i in range(3):
            gshort_ref[i, :, 128 * jt : 128 * (jt + 1)] = total[TAPS * i : TAPS * (i + 1), :]

    for copy in keep_out:
        copy.wait()
    most = pl.ds(0, HALF - 1)
    arrived(so.at[most, 0], 6)
    arrived(so.at[most, 1], 7)
    arrived(so.at[most, pl.ds(2, 2)], 8)
    left(rx.at[most, pl.ds(1, 2)], 0)
    left(rx.at[most, 0], 1)
    left(rx.at[most, 3], 2)
    left(filt.at[pl.ds(0, 3)], 3)
    left(edge.at[0], 4)
    left(edge.at[1], 5)
    left(so.at[most, 0], 6)
    left(so.at[most, 1], 7)
    left(so.at[most, pl.ds(2, 2)], 8)
    left(sums.at[0, pl.ds(0, 16)], 9)
    left(sums.at[1], 10)
    left(all_short.at[most], 11)


def per_device(projected, short_weight, residues, decay_rates, skip_weight, cotangent):
    n = lax.axis_size("context")
    channels, local_len = cotangent.shape
    own = channels // n
    steps = local_len // SUB
    vmem = pl.BlockSpec(memory_space=pltpu.VMEM)
    anywhere = pl.BlockSpec(memory_space=pl.ANY)
    stepped = pltpu.VMEM((RUNS, steps, SUB, 128), F32)
    blocks = (RUNS, 2, WIDE, own, local_len)
    results = pl.pallas_call(
        functools.partial(kernel, n, local_len, own),
        out_shape=(
            jax.ShapeDtypeStruct(blocks, BF16),
            jax.ShapeDtypeStruct((3,) + blocks, BF16),
            jax.ShapeDtypeStruct((3, TAPS, channels), F32),
            jax.ShapeDtypeStruct((own, MODES), F32),
            jax.ShapeDtypeStruct((own, MODES), F32),
            jax.ShapeDtypeStruct((1, own), F32),
        ),
        in_specs=[anywhere] * 6,
        out_specs=(anywhere, anywhere, vmem, vmem, vmem, vmem),
        scratch_shapes=[
            pltpu.VMEM((HALF, 4, 2, own, local_len), BF16),
            pltpu.VMEM((HALF, 4, 2, own, local_len), BF16),
            pltpu.VMEM((4, RUNS, OFF + local_len, 128), F32),
            stepped,
            stepped,
            stepped,
            stepped,
            stepped,
            stepped,
            pltpu.VMEM((3, RUNS, local_len + 8, 128), F32),
            pltpu.VMEM((RUNS, local_len, 128), F32),
            pltpu.VMEM((3, TAPS, channels), F32),
            pltpu.VMEM((6, own, MODES), F32),
            pltpu.VMEM((4, 128, 128), F32),
            pltpu.VMEM((10, SUB, 128), F32),
            pltpu.VMEM((MODES, SUB, 128), F32),
            pltpu.VMEM((MODES, SUB, 128), F32),
            pltpu.VMEM((2, RUNS, MODES, 128), F32),
            pltpu.VMEM((2, RUNS, MODES, SUB, 128), F32),
            pltpu.VMEM((RUNS, MODES, 128), F32),
            pltpu.VMEM((2, MODES + 8, 128), F32),
            pltpu.VMEM((2, MODES + 8, 128), F32),
            pltpu.VMEM((2, 2 * MODES, 128), F32),
            pltpu.VMEM((2, 2 * MODES, 128), F32),
            pltpu.VMEM((16, 128), F32),
            pltpu.VMEM((HALF, 16, 128), F32),
            pltpu.VMEM((MODES, SUB, 128), F32),
            pltpu.VMEM((MODES, SUB, 128), F32),
            pltpu.SemaphoreType.DMA((12,)),
            pltpu.SemaphoreType.DMA((12,)),
            pltpu.SemaphoreType.DMA((6,)),
        ],
        compiler_params=pltpu.CompilerParams(
            collective_id=0, has_side_effects=True, vmem_limit_bytes=56 * 1024 * 1024
        ),
    )(
        projected.reshape((3,) + blocks),
        cotangent.reshape(blocks),
        short_weight.transpose(0, 2, 1),
        decay_rates,
        residues,
        skip_weight.reshape(1, -1),
    )
    output, grad_projected, grad_short, grad_res, grad_dec, grad_skip = results
    return (
        output.reshape(channels, local_len),
        grad_projected.reshape(3, channels, local_len),
        grad_short.transpose(0, 2, 1),
        grad_res,
        grad_dec,
        grad_skip.reshape(-1),
    )


def solution(mesh):
    return jax.shard_map(
        per_device,
        mesh=mesh,
        in_specs=(
            P(None, "tensor", "context"),
            P(None, "tensor", None),
            P(("tensor", "context"), None),
            P(("tensor", "context"), None),
            P(("tensor", "context")),
            P("tensor", "context"),
        ),
        out_specs=(
            P("tensor", "context"),
            P(None, "tensor", "context"),
            P(None, "tensor", None),
            P(("tensor", "context"), None),
            P(("tensor", "context"), None),
            P(("tensor", "context")),
        ),
        check_vma=False,
    )
```

time: 254 us -> 43.9 us (0.17); the launches traced: 249 us -> 43.6 us
  blocking collectives: 129 us -> 0 us
  Pallas kernels: 0 us -> 37 us
  matrix products: 31.6 us -> 0 us
  starting transfers between devices: 29.8 us -> 0 us
  other arithmetic: 20 us -> 0 us
  waiting for transfers between devices: 17.6 us -> 0 us
  local copies, waits for them, and re-layouts: 18.7 us -> 5.92 us
    psum x1 -> x0, blocking collectives: 129 us -> none  [per_device(): grad_short = lax.psum(partial_taps, 'context') / math.sqrt(length)]
    pallas_call x0 -> x1, Pallas kernels: none -> 37 us  [per_device(): pl.pallas_call(functools.partial(kernel, n, local_len, own), out_shape=(j...]
    dot_general x36 -> x0, matrix products: 31.6 us -> none  [the longest x24 19.7 us: inner_product(): return jnp.einsum('ckb,bm->ckm', left, table, precision=PRECISE)]
    all_to_all x4 -> x0, starting transfers between devices: 22.5 us -> none  [the longest x1 8.15 us: per_device(): lax.all_to_all(gated_signal, 'context', split_axis=0, concat_axis=1, tile...]
    all_to_all x4 -> x0, waiting for transfers between devices: 15.4 us -> none  [the longest x1 5.76 us: per_device(): lax.all_to_all(gated_signal, 'context', split_axis=0, concat_axis=1, tile...]
    div x6 -> x0, local copies, waits for them, and re-layouts: 9.41 us -> none  [inverse_dft(): return blocks.reshape(channels, -1) / total]
    reduce_sum x18 -> x0, other arithmetic: 9.4 us -> none  [the longest x16 4.16 us: one_mode(): plain = jnp.sum(grad_filter * weights, axis=1)]
    ppermute x2 -> x0, starting transfers between devices: 7.24 us -> none  [passed_along(): return lax.ppermute(block, axis, route)]
  transfers between devices with their start and end apart: 6 -> 0, of which waited for: 5 -> 0; matrix products, arithmetic and copies ran while one was open for 11% -> 0% of each run, Pallas kernels for 0% -> 0%
where the time goes in v2:
time: 43.9 us; the launch traced here: 43.6 us
  Pallas kernels  37 us (84%)
  local copies, waits for them, and re-layouts  5.92 us (13%)
  between operations  0.65 us (1%)
    pallas_call x1, Pallas kernels, per_device(): pl.pallas_call(functools.partial(kernel, n, local_len, own), out_shape=(j...  37 us
    unnamed x14, local copies, waits for them, and re-layouts  5.92 us

profile of v2, /device:TPU:1, one launch (start us, length us, event | category | flops | bytes accessed | tf_op | source)
XLA Modules:
  0.0 43.6 jit_solution(2955342418376909188)
XLA Ops:
  0.6 37.0 %shard_map.109 = (bf16[4,2,4,16,128]{4,3,2,1,0:T(8,128)(2,1)}, bf16[3,4,2,4,16,128]{5,4,3,2,1,0:T(8,128)(2,1)}, f32[3,3,512]{2,1,0:T(4,128)}, f32[16,16]{1,0:T(8...) custom-call(bf16[3,4,2,4,16,128]{5,4,3,2,1,0:T(8,128)(2,1)} %bitcast.8, bf16[4,2,4,16,128]{4,3,2,1,0:T(8,128)(2,1)} %bitcast.10, ...), custom_call_target="tpu_custom_call" | custom-call | tf_op jit(solution)/shard_map/pallas_call | solution.py:718
  37.7 1.6 %copy.18 = bf16[512,128]{1,0:T(8,128)(2,1)} copy(bf16[512,128]{1,0:T(8,128)(2,1)} %bitcast.11) | data formatting | bytes 262144
  39.2 0.0 copy-start
  39.2 1.8 %copy.19 = bf16[3,512,128]{2,1,0:T(8,128)(2,1)} copy(bf16[3,512,128]{2,1,0:T(8,128)(2,1)} %bitcast.9) | data formatting | bytes 786432
  41.0 0.0 copy-done
  41.0 0.0 copy-start.2
  41.0 0.6 %copy.20 = f32[3,512,3]{1,2,0:T(4,128)} copy(f32[3,512,3]{1,2,0:T(4,128)S(1)} %bitcast.13) | data formatting | bytes 36864
  41.6 0.1 copy-done.2
  41.7 0.0 copy-start.1
  41.7 0.6 %copy.21 = f32[16,16]{1,0:T(8,128)} copy(f32[16,16]{1,0:T(8,128)S(1)} %copy-done.2) | data formatting | bytes 2048
  42.3 0.1 copy-done.1
  42.4 0.0 copy-start.3
  42.4 0.6 %copy.22 = f32[16,16]{1,0:T(8,128)} copy(f32[16,16]{1,0:T(8,128)S(1)} %copy-done.1) | data formatting | bytes 2048
  43.0 0.1 copy-done.3
  43.1 0.5 %copy.23 = f32[16]{0:T(128)} copy(f32[16]{0:T(128)S(1)} %bitcast.15) | data formatting | bytes 128
Async XLA Ops:
  39.2 1.8 %copy-start = (f32[3,3,512]{2,1,0:T(4,128)S(1)}, f32[3,3,512]{2,1,0:T(4,128)}, u32[]{:S(2)}) copy-start(f32[3,3,512]{2,1,0:T(4,128)} %get-tuple-element.14) | copy-start | bytes 55300
  41.0 0.7 %copy-start.2 = (f32[16,16]{1,0:T(8,128)S(1)}, f32[16,16]{1,0:T(8,128)}, u32[]{:S(2)}) copy-start(f32[16,16]{1,0:T(8,128)} %get-tuple-element.27) | copy-start | bytes 3076
  41.7 0.7 %copy-start.1 = (f32[16,16]{1,0:T(8,128)S(1)}, f32[16,16]{1,0:T(8,128)}, u32[]{:S(2)}) copy-start(f32[16,16]{1,0:T(8,128)} %get-tuple-element.28) | copy-start | bytes 3076
  42.4 0.7 %copy-start.3 = (f32[1,16]{1,0:T(1,128)S(1)}, f32[1,16]{1,0:T(1,128)}, u32[]{:S(2)}) copy-start(f32[1,16]{1,0:T(1,128)} %get-tuple-element.17) | copy-start | bytes 196

commit v3 on v2

--- a/solution.py
+++ b/solution.py
@@ -12,7 +12,7 @@
 SUB = 8
 MODES = 16
 TAPS = 3
-OFF = 8
+RIM = TAPS - 1
 RUNS = 4
 WIDE = 4
 HALF = RUNS * WIDE
@@ -42,7 +42,6 @@
     res_hbm,
     skip_hbm,
     out_ref,
-    gproj_ref,
     gshort_ref,
     gres_ref,
     gdec_ref,
@@ -57,7 +56,7 @@
     gs,
     cv,
     gf,
-    ot,
+    kept,
     sw,
     filt,
     par,
@@ -236,34 +235,61 @@
     up_span = jnp.exp(per * (-1.0 * local_len) * group.astype(F32))
     down_span = jnp.exp(per * (-1.0 * local_len) * (WIDE - 1 - group).astype(F32))
 
+    row = lax.broadcasted_iota(jnp.int32, (local_len, local_len), 0)
+    column = lax.broadcasted_iota(jnp.int32, (local_len, local_len), 1)
+    order = jnp.where(column == lax.rem(row, SUB) * steps + row // SUB, 1.0, 0.0).astype(BF16)
+
     def turn(arrays):
         def tile(jt, carry):
             for a in arrays:
-                block = rx[pl.ds(WIDE * jt, WIDE), a].reshape(128, local_len).astype(F32)
-                turned = block.T
-                xt[a, jt, OFF : OFF + local_len, :] = turned
+                block = rx[pl.ds(WIDE * jt, WIDE), a].reshape(128, local_len)
+                rows = lax.dot_general(
+                    order, block, (((1,), (1,)), ((), ())), preferred_element_type=F32
+                ).reshape(steps, SUB, 128)
+                xt[a, jt, RIM : RIM + steps] = rows
                 if a < 3:
-                    xt[a, jt, 0:OFF, :] = jnp.where(
-                        group == 0, 0.0, pltpu.roll(turned[local_len - OFF :, :], chans, 1)
-                    )
+                    for i in range(RIM):
+                        moved = pltpu.roll(rows[steps - RIM + i], 1, 0)
+                        first = jnp.where(group == 0, 0.0, pltpu.roll(moved, chans, 1))
+                        xt[a, jt, i] = jnp.where(sub_row == 0, first, moved)
             return carry
 
         lax.fori_loop(0, RUNS, tile, 0)
+
+    def turn_back(rows):
+        flat = rows.astype(BF16).reshape(local_len, 128)
+        return (
+            lax.dot_general(flat, order, (((0,), (0,)), ((), ())), preferred_element_type=F32)
+            .astype(BF16)
+            .reshape(WIDE, 2, own, local_len)
+        )
 
     def path(a, jt, p):
         total = None
         for j in range(TAPS):
-            term = wt[TAPS * a + j] * xt[a, jt, pl.ds(OFF + p - j, SUB, stride=steps), :]
+            term = wt[TAPS * a + j] * xt[a, jt, RIM + p - j]
             total = term if total is None else total + term
         return total
 
     def last_rows(a):
         return packed(
-            [xt[a, jt, OFF + local_len - 8 : OFF + local_len, :] for jt in range(RUNS)], WIDE - 1
-        )[6:8, :]
+            [
+                jnp.concatenate(
+                    [xt[a, jt, steps + i, SUB - 1 : SUB, :] for i in range(RIM)], axis=0
+                )
+                for jt in range(RUNS)
+            ],
+            WIDE - 1,
+        )
 
     def first_rows(a):
-        return packed([xt[a, jt, OFF : OFF + 8, :] for jt in range(RUNS)], 0)[0:2, :]
+        return packed(
+            [
+                jnp.concatenate([xt[a, jt, RIM + i, 0:1, :] for i in range(RIM)], axis=0)
+                for jt in range(RUNS)
+            ],
+            0,
+        )
 
     def edge_path(a, first, last):
         w = [wt[TAPS * a + j][0:1, :] for j in range(TAPS)]
@@ -284,7 +310,10 @@
     def fill_rim(a, rows):
         for jt in range(RUNS):
             rim = to_group(rows, jt, 0)
-            xt[a, jt, OFF - 2 : OFF, :] = jnp.where(group == 0, rim, xt[a, jt, OFF - 2 : OFF, :])
+            for i in range(RIM):
+                xt[a, jt, i] = jnp.where(
+                    corner, jnp.broadcast_to(rim[i : i + 1, :], (SUB, 128)), xt[a, jt, i]
+                )
 
     many = 8
 
@@ -362,20 +391,23 @@
     def gate_q(jt, carry):
         for p in range(steps):
             query = path(0, jt, p)
-            g = rounded(xt[3, jt, pl.ds(OFF + p, SUB, stride=steps), :] * query)
+            g = rounded(xt[3, jt, RIM + p] * query)
             qs[jt, p] = query
             gs[jt, p] = jnp.where(corner, 0.0, g) if p < 2 else g
         return carry
 
+    q_last, q_first, c_first = last_rows(0), first_rows(0), first_rows(3)
+    edge[1, MODES : MODES + 8, :] = jnp.concatenate(
+        [q_last, q_first, c_first, jnp.zeros((2, 128), F32)], axis=0
+    )
+    remote(
+        edge.at[1, pl.ds(MODES, 8)], edge_in.at[1, pl.ds(MODES, 8)], 10, partner
+    ).start()
     lax.fori_loop(0, RUNS, gate_q, 0)
     block_ends(1, gs, True)
     my_b = run_ends(1, True)
-    q_last, q_first, c_first = last_rows(0), first_rows(0), first_rows(3)
     edge[1, 0:MODES, :] = my_b
-    edge[1, MODES : MODES + 8, :] = jnp.concatenate(
-        [q_last, q_first, c_first, jnp.zeros((2, 128), F32)], axis=0
-    )
-    remote(edge.at[1], edge_in.at[1], 5, partner).start()
+    remote(edge.at[1, pl.ds(0, MODES)], edge_in.at[1, pl.ds(0, MODES)], 5, partner).start()
 
     arrived(edge_in.at[0], 4)
     their_f = edge_in[0, 0:MODES, :]
@@ -424,40 +456,35 @@
             state = jnp.where(corner, exact, state)
         return state
 
-    def filtered_by_modes(k, signal, jt):
+    def summed(parts):
+        while len(parts) > 1:
+            parts = [parts[i] + parts[i + 1] for i in range(0, len(parts), 2)]
+        return parts[0]
+
+    def conv_tile(jt, carry):
         def some(at, totals):
             totals = list(totals)
             first = at * many
             lams = [lam[first + i] for i in range(many)]
             coefs = [coef[first + i] for i in range(many)]
-            state = [in_state(k, jt, first + i) for i in range(many)]
-            for i in range(many):
-                ins[k, jt, first + i] = state[i]
-            for p in reversed(range(steps)) if k else range(steps):
-                x = signal[jt, p]
-                parts = []
+            state = [in_state(0, jt, first + i) for i in range(many)]
+            for p in range(steps):
+                u = us[jt, p]
                 for i in range(many):
-                    state[i] = lams[i] * state[i] + x
-                    parts.append(coefs[i] * state[i])
-                while len(parts) > 1:
-                    parts = [parts[i] + parts[i + 1] for i in range(0, len(parts), 2)]
-                totals[p] = totals[p] + parts[0]
+                    state[i] = lams[i] * state[i] + u
+                    kept[jt, first + i, p] = state[i]
+                totals[p] = totals[p] + summed([coefs[i] * state[i] for i in range(many)])
             return tuple(totals)
 
-        skip = wt[9]
-        start = tuple(skip * signal[jt, p] for p in range(steps))
-        return lax.fori_loop(0, MODES // many, some, start)
-
-    def conv_tile(jt, carry):
-        totals = filtered_by_modes(0, us, jt)
+        start = tuple(wt[9] * us[jt, p] for p in range(steps))
+        totals = lax.fori_loop(0, MODES // many, some, start)
         for p in range(steps):
             cv[jt, p] = rounded(totals[p])
         return carry
 
     lax.fori_loop(0, RUNS, conv_tile, 0)
 
-    arrived(edge_in.at[1], 5)
-    their_b = edge_in[1, 0:MODES, :]
+    arrived(edge_in.at[1, pl.ds(MODES, 8)], 10)
     rows = edge_in[1, MODES : MODES + 8, :]
     tq_last, tq_first, tc_first = rows[0:2], rows[2:4], rows[4:6]
     fill_rim(0, theirs_before(tq_last))
@@ -466,33 +493,73 @@
         for p in range(2):
             query = path(0, jt, p)
             qs[jt, p] = query
-            gs[jt, p] = rounded(xt[3, jt, pl.ds(OFF + p, SUB, stride=steps), :] * query)
+            gs[jt, p] = rounded(xt[3, jt, RIM + p] * query)
+        for p in range(steps):
+            gf[0, jt, p] = xt[3, jt, RIM + p] * cv[jt, p]
         return carry
 
     lax.fori_loop(0, RUNS, regate_q, 0)
-
-    def output_tile(jt, carry):
+    next_u = [theirs_after(u) for u in their_u]
+    next_c = theirs_after(tc_first)
+    state0 = lam_rows * next_f + next_u[0]
+    state1 = lam_rows * state0 + next_u[1]
+    beyond = [[], [], []]
+    for i, state in enumerate((state0, state1)):
+        conv = rounded(
+            jnp.sum(coef_rows * state, axis=0, keepdims=True) + skip_row * next_u[i]
+        )
+        beyond[0].append(next_c[i : i + 1] * conv)
+
+    def gf_rim(a):
+        for jt in range(RUNS):
+            for i in range(RIM):
+                rim = jnp.broadcast_to(to_group(beyond[a][i], jt, WIDE - 1), (SUB, 128))
+                moved = pltpu.roll(gf[a, jt, i], SUB - 1, 0)
+                last = jnp.where(group == WIDE - 1, rim, pltpu.roll(moved, 128 - chans, 1))
+                gf[a, jt, steps + i] = jnp.where(sub_row == SUB - 1, last, moved)
+
+    def grad_path(a, jt):
+        w = [wt[TAPS * a + j] for j in range(TAPS)]
+        rows = []
         for p in range(steps):
-            at = pl.ds(p, SUB, stride=steps)
-            conv = cv[jt, p]
-            ot[jt, at, :] = qs[jt, p] * conv
-            gf[0, jt, at, :] = xt[3, jt, pl.ds(OFF + p, SUB, stride=steps), :] * conv
-        so[pl.ds(WIDE * jt, WIDE), 0] = (
-            ot[jt].T.astype(BF16).reshape(WIDE, 2, own, local_len)
-        )
+            total = w[0] * gf[a, jt, p]
+            for j in range(1, TAPS):
+                total = total + w[j] * gf[a, jt, p + j]
+            rows.append(total)
+        so[pl.ds(WIDE * jt, WIDE), 1 + a] = turn_back(jnp.stack(rows))
+
+    def send_tile(jt, arrays, k):
+        for w in range(WIDE):
+            slot = WIDE * jt + w
+
+            @pl.when(slot != my_slot)
+            def _():
+                remote(
+                    so.at[slot, arrays],
+                    out_ref.at[arrays, my_x, :, my_w],
+                    k,
+                    (2 * jt + side) * WIDE + w,
+                ).start()
+
+    gf_rim(0)
+
+    def first_results(t, carry):
+        jt = lax.rem(my_x + 1 + t, RUNS)
+        so[pl.ds(WIDE * jt, WIDE), 0] = turn_back(
+            jnp.stack([qs[jt, p] * cv[jt, p] for p in range(steps)])
+        )
+        grad_path(0, jt)
+        send_tile(jt, pl.ds(0, 2), 7)
         return carry
 
-    lax.fori_loop(0, RUNS, output_tile, 0)
-
-    def send_out(slot, x, w, device):
-        remote(so.at[slot, 0], out_ref.at[my_x, :, my_w], 6, device).start()
-
-    each_peer(send_out)
+    lax.fori_loop(0, RUNS, first_results, 0)
 
     my_q = edge_path(0, q_first, theirs_before(tq_last))
     their_q = edge_path(0, tq_first, mine_before(q_last))
     my_g = [rounded(my_q[i] * c_first[i : i + 1]) for i in range(2)]
     their_g = [rounded(their_q[i] * tc_first[i : i + 1]) for i in range(2)]
+    arrived(edge_in.at[1, pl.ds(0, MODES)], 5)
+    their_b = edge_in[1, 0:MODES, :]
     my_b = my_b + my_g[0] + lam_rows * my_g[1]
     their_b = their_b + their_g[0] + lam_rows * their_g[1]
     a_b, b_b = jnp.where(is_a, my_b, their_b), jnp.where(is_a, their_b, my_b)
@@ -506,170 +573,123 @@
     for jt in range(RUNS):
         tots[1, jt] = tots[1, jt] + down_span * repeated(carry_b, jt)
 
-    next_u = [theirs_after(u) for u in their_u]
     next_g = [theirs_after(g) for g in their_g]
-    state0 = lam_rows * next_f + next_u[0]
-    state1 = lam_rows * state0 + next_u[1]
-    back0 = carry_b
-    back1 = inv_lam * (carry_b - next_g[0])
-    beyond = [[], [], []]
-    for i, (state, back) in enumerate(((state0, back0), (state1, back1))):
-        conv = rounded(
-            jnp.sum(coef_rows * state, axis=0, keepdims=True) + skip_row * next_u[i]
-        )
+    for i, back in enumerate((carry_b, inv_lam * (carry_b - next_g[0]))):
         back = rounded(jnp.sum(coef_rows * back, axis=0, keepdims=True) + skip_row * next_g[i])
-        beyond[0].append(theirs_after(tc_first[i : i + 1]) * conv)
         beyond[1].append(back * theirs_after(their_v[i]))
         beyond[2].append(back * theirs_after(their_k[i]))
 
-    def gf_rim(a):
-        rows = jnp.concatenate(beyond[a] + [jnp.zeros((6, 128), F32)], axis=0)
-        for jt in range(RUNS):
-            inner = pltpu.roll(gf[a, jt, 0:8, :], 128 - chans, 1)
-            gf[a, jt, local_len : local_len + 8, :] = jnp.where(
-                group == WIDE - 1, to_group(rows, jt, WIDE - 1), inner
-            )
-
-    def grad_path(a, jt):
-        total = None
-        for j in range(TAPS):
-            w = jnp.broadcast_to(wt[TAPS * a + j][0:1, :], (local_len, 128))
-            term = w * gf[a, jt, j : j + local_len, :]
-            total = term if total is None else total + term
-        so[pl.ds(WIDE * jt, WIDE), 1 + a] = (
-            total.T.astype(BF16).reshape(WIDE, 2, own, local_len)
-        )
-
-    def grad_taps(a, jt):
-        return [
-            jnp.sum(
-                gf[a, jt, 0:local_len, :] * xt[a, jt, OFF - j : OFF - j + local_len, :],
-                axis=0,
-                keepdims=True,
-            )
-            for j in range(TAPS)
-        ]
-
-    gf_rim(0)
-
-    def grad_q_tile(jt, carry):
-        grad_path(0, jt)
-        return carry
-
-    lax.fori_loop(0, RUNS, grad_q_tile, 0)
-
-    def send_gq(slot, x, w, device):
-        remote(so.at[slot, 1], gproj_ref.at[0, my_x, :, my_w], 7, device).start()
-
-    each_peer(send_gq)
-
-    def back_tile(jt, skip_total):
-        totals = filtered_by_modes(1, gs, jt)
+    def back_tile(jt, carry):
+        def some(at, totals):
+            totals = list(totals)
+            first = at * many
+            lams = [lam[first + i] for i in range(many)]
+            coefs = [coef[first + i] for i in range(many)]
+            state = [in_state(1, jt, first + i) for i in range(many)]
+            for i in range(many):
+                ins[1, jt, first + i] = state[i]
+            for p in reversed(range(steps)):
+                g = gs[jt, p]
+                for i in range(many):
+                    state[i] = lams[i] * state[i] + g
+                totals[p] = totals[p] + summed([coefs[i] * state[i] for i in range(many)])
+            return tuple(totals)
+
+        carry = list(carry)
+        start = tuple(wt[9] * gs[jt, p] for p in range(steps))
+        totals = lax.fori_loop(0, MODES // many, some, start)
         for p in range(steps):
-            at = pl.ds(p, SUB, stride=steps)
             back = rounded(totals[p])
-            gf[1, jt, at, :] = back * vs[jt, p]
-            gf[2, jt, at, :] = back * ks[jt, p]
-            skip_total = skip_total + us[jt, p] * gs[jt, p]
-        return skip_total
-
-    skip_total = lax.fori_loop(0, RUNS, back_tile, jnp.zeros((SUB, 128), F32))
+            grads = (gf[0, jt, p], back * vs[jt, p], back * ks[jt, p])
+            gf[1, jt, p] = grads[1]
+            gf[2, jt, p] = grads[2]
+            for a in range(3):
+                for j in range(TAPS):
+                    carry[TAPS * a + j] += grads[a] * xt[a, jt, RIM + p - j]
+            carry[9] += us[jt, p] * gs[jt, p]
+        return tuple(carry)
+
+    found = lax.fori_loop(
+        0, RUNS, back_tile, tuple(jnp.zeros((SUB, 128), F32) for _ in range(10))
+    )
+
+    rows = jnp.concatenate(
+        [jnp.sum(part, axis=0, keepdims=True) for part in found] + [jnp.zeros((6, 128), F32)],
+        axis=0,
+    )
+    my_short = group_sum(rows) * (1.0 / root)
+    sums[0:16, :] = my_short
+    remote(sums.at[pl.ds(0, 16)], sums_in.at[pl.ds(0, 16)], 6, partner).start()
+
     gf_rim(1)
     gf_rim(2)
 
-    def grad_kv_tile(jt, carry):
+    def last_results(t, carry):
+        jt = lax.rem(my_x + 1 + t, RUNS)
         grad_path(1, jt)
         grad_path(2, jt)
+        send_tile(jt, pl.ds(2, 2), 8)
         return carry
 
-    lax.fori_loop(0, RUNS, grad_kv_tile, 0)
-
-    def send_gkv(slot, x, w, device):
-        remote(
-            so.at[slot, pl.ds(2, 2)], gproj_ref.at[pl.ds(1, 2), my_x, :, my_w], 8, device
-        ).start()
-
-    each_peer(send_gkv)
-    keep_out = [
-        pltpu.make_async_copy(so.at[my_slot, 0], out_ref.at[my_x, :, my_w], local_sem.at[0]),
-        pltpu.make_async_copy(
-            so.at[my_slot, pl.ds(1, 3)], gproj_ref.at[:, my_x, :, my_w], local_sem.at[1]
-        ),
-    ]
-    for copy in keep_out:
-        copy.start()
-
-    def taps_tile(jt, carry):
-        found = [part for a in range(3) for part in grad_taps(a, jt)]
-        return tuple(c + f for c, f in zip(carry, found))
-
-    found = lax.fori_loop(0, RUNS, taps_tile, tuple(jnp.zeros((1, 128), F32) for _ in range(9)))
-    rows = jnp.concatenate(
-        list(found)
-        + [jnp.sum(skip_total, axis=0, keepdims=True), jnp.zeros((6, 128), F32)],
-        axis=0,
-    )
-    my_short = group_sum(rows) * (1.0 / root)
-    sums[0, 0:16, :] = my_short
-    remote(sums.at[0, pl.ds(0, 16)], sums_in.at[0, pl.ds(0, 16)], 9, partner).start()
+    lax.fori_loop(0, RUNS, last_results, 0)
+    keep_out = pltpu.make_async_copy(so.at[my_slot], out_ref.at[:, my_x, :, my_w], local_sem.at[0])
+    keep_out.start()
 
     pacc[...] = jnp.zeros_like(pacc)
     racc[...] = jnp.zeros_like(racc)
-    pair = 2
+    few = 4
 
     def mode_sums(at, carry):
-        jt = at // (MODES // pair)
-        first = lax.rem(at, MODES // pair) * pair
-        lams = [lam[first + i] for i in range(pair)]
-        behind = [[None] * steps + [ins[1, jt, first + i]] for i in range(pair)]
-        for p in reversed(range(1, steps)):
+        jt = at // (MODES // few)
+        first = lax.rem(at, MODES // few) * few
+        lams = [lam[first + i] for i in range(few)]
+        state = [ins[1, jt, first + i] for i in range(few)]
+        plain = [None] * few
+        ramped = [None] * few
+        for p in reversed(range(steps)):
             g = gs[jt, p]
-            for i in range(pair):
-                behind[i][p] = lams[i] * behind[i][p + 1] + g
-        plain = [None] * pair
-        ramped = [None] * pair
-        state = [ins[0, jt, first + i] for i in range(pair)]
-        for p in range(steps):
-            u = us[jt, p]
-            g = gs[jt, p]
-            for i in range(pair):
-                state[i] = lams[i] * state[i] + u
-                flat = g * state[i]
-                ramp = behind[i][p + 1] * state[i]
+            for i in range(few):
+                fwd = kept[jt, first + i, p]
+                flat = g * fwd
+                ramp = state[i] * fwd
                 plain[i] = flat if plain[i] is None else plain[i] + flat
                 ramped[i] = ramp if ramped[i] is None else ramped[i] + ramp
-        for i in range(pair):
+                state[i] = lams[i] * state[i] + g
+        for i in range(few):
             pacc[first + i] += plain[i]
             racc[first + i] += ramped[i]
         return carry
 
-    lax.fori_loop(0, RUNS * (MODES // pair), mode_sums, 0)
+    lax.fori_loop(0, RUNS * (MODES // few), mode_sums, 0)
     my_plain = group_sum(
         jnp.concatenate([jnp.sum(pacc[m], axis=0, keepdims=True) for m in range(MODES)], axis=0)
     )
     my_ramped = group_sum(
         jnp.concatenate([jnp.sum(racc[m], axis=0, keepdims=True) for m in range(MODES)], axis=0)
     )
-    sums[1, 0:MODES, :] = my_plain
-    sums[1, MODES : 2 * MODES, :] = my_ramped
-    remote(sums.at[1], sums_in.at[1], 10, partner).start()
-
-    arrived(sums_in.at[0, pl.ds(0, 16)], 9)
-    short = my_short + sums_in[0, 0:16, :]
+    sums[16 : 16 + MODES, :] = my_plain
+    sums[16 + MODES : 16 + 2 * MODES, :] = my_ramped
+    remote(
+        sums.at[pl.ds(16, 2 * MODES)], sums_in.at[pl.ds(16, 2 * MODES)], 11, partner
+    ).start()
+
+    arrived(sums_in.at[pl.ds(0, 16)], 6)
+    short = my_short + sums_in[0:16, :]
     odd = lax.rem(my_w, 2) == 1
     other = pltpu.roll(short, own, 1)
-    low, high = jnp.where(odd, other, short), jnp.where(odd, short, other)
+    low = jnp.where(odd, other, short)[0:9, :]
+    high = jnp.where(odd, short, other)[0:9, :]
     place = lane // own
     shorts[...] = jnp.where(place == my_w, low, jnp.where(place == my_w + WIDE, high, 0.0))
     each_peer(
-        lambda slot, x, w, device: remote(shorts, all_short.at[my_slot], 11, device).start()
+        lambda slot, x, w, device: remote(shorts, all_short.at[my_slot], 9, device).start()
     )
     all_short[my_slot] = shorts[...]
     gskip_ref[...] = jnp.where(is_a, short[9:10, 0:own], short[9:10, own : 2 * own])
 
-    arrived(sums_in.at[1], 10)
-    plain = my_plain + sums_in[1, 0:MODES, :]
-    ramped = lam_rows * (my_ramped + sums_in[1, MODES : 2 * MODES, :])
+    arrived(sums_in.at[pl.ds(16, 2 * MODES)], 11)
+    plain = my_plain + sums_in[16 : 16 + MODES, :]
+    ramped = lam_rows * (my_ramped + sums_in[16 + MODES : 16 + 2 * MODES, :])
     grad_res = scale * plain / root
     grad_dec = residue * (jnp.exp(-2.0 * per) / scale * plain - scale * ramped) / (length * root)
     par[0, 0:MODES, :] = grad_res
@@ -678,7 +698,7 @@
         turned = par[k].T
         ref[...] = jnp.where(is_a, turned[0:own, 0:MODES], turned[own : 2 * own, 0:MODES])
 
-    arrived(all_short.at[pl.ds(0, HALF - 1)], 11)
+    arrived(all_short.at[pl.ds(0, HALF - 1)], 9)
     for jt in range(RUNS):
         total = all_short[WIDE * jt]
         for w in range(1, WIDE):
@@ -686,24 +706,31 @@
         for i in range(3):
             gshort_ref[i, :, 128 * jt : 128 * (jt + 1)] = total[TAPS * i : TAPS * (i + 1), :]
 
-    for copy in keep_out:
-        copy.wait()
+    keep_out.wait()
     most = pl.ds(0, HALF - 1)
-    arrived(so.at[most, 0], 6)
-    arrived(so.at[most, 1], 7)
+    arrived(so.at[most, pl.ds(0, 2)], 7)
     arrived(so.at[most, pl.ds(2, 2)], 8)
     left(rx.at[most, pl.ds(1, 2)], 0)
     left(rx.at[most, 0], 1)
     left(rx.at[most, 3], 2)
     left(filt.at[pl.ds(0, 3)], 3)
     left(edge.at[0], 4)
-    left(edge.at[1], 5)
-    left(so.at[most, 0], 6)
-    left(so.at[most, 1], 7)
+    left(edge.at[1, pl.ds(0, MODES)], 5)
+    left(edge.at[1, pl.ds(MODES, 8)], 10)
+    left(sums.at[pl.ds(0, 16)], 6)
+    left(sums.at[pl.ds(16, 2 * MODES)], 11)
+    left(so.at[most, pl.ds(0, 2)], 7)
     left(so.at[most, pl.ds(2, 2)], 8)
-    left(sums.at[0, pl.ds(0, 16)], 9)
-    left(sums.at[1], 10)
-    left(all_short.at[most], 11)
+    left(all_short.at[most], 9)
+
+
+def write_out(paths, short, res, dec, skip, out, gproj, gshort, gres, gdec, gskip):
+    out[...] = paths[0]
+    gproj[...] = paths[1:]
+    gshort[...] = short[...]
+    gres[...] = res[...]
+    gdec[...] = dec[...]
+    gskip[...] = skip[...]
 
 
 def per_device(projected, short_weight, residues, decay_rates, skip_weight, cotangent):
@@ -712,33 +739,32 @@
     own = channels // n
     steps = local_len // SUB
     vmem = pl.BlockSpec(memory_space=pltpu.VMEM)
-    anywhere = pl.BlockSpec(memory_space=pl.ANY)
+    hbm = pl.BlockSpec(memory_space=pltpu.HBM)
     stepped = pltpu.VMEM((RUNS, steps, SUB, 128), F32)
     blocks = (RUNS, 2, WIDE, own, local_len)
+    small = (
+        jax.ShapeDtypeStruct((3, TAPS, channels), F32),
+        jax.ShapeDtypeStruct((own, MODES), F32),
+        jax.ShapeDtypeStruct((own, MODES), F32),
+        jax.ShapeDtypeStruct((1, own), F32),
+    )
     results = pl.pallas_call(
         functools.partial(kernel, n, local_len, own),
-        out_shape=(
-            jax.ShapeDtypeStruct(blocks, BF16),
-            jax.ShapeDtypeStruct((3,) + blocks, BF16),
-            jax.ShapeDtypeStruct((3, TAPS, channels), F32),
-            jax.ShapeDtypeStruct((own, MODES), F32),
-            jax.ShapeDtypeStruct((own, MODES), F32),
-            jax.ShapeDtypeStruct((1, own), F32),
-        ),
-        in_specs=[anywhere] * 6,
-        out_specs=(anywhere, anywhere, vmem, vmem, vmem, vmem),
+        out_shape=(jax.ShapeDtypeStruct((4,) + blocks, BF16),) + small,
+        in_specs=[hbm] * 6,
+        out_specs=(vmem,) * 5,
         scratch_shapes=[
             pltpu.VMEM((HALF, 4, 2, own, local_len), BF16),
             pltpu.VMEM((HALF, 4, 2, own, local_len), BF16),
-            pltpu.VMEM((4, RUNS, OFF + local_len, 128), F32),
+            pltpu.VMEM((4, RUNS, RIM + steps, SUB, 128), F32),
             stepped,
             stepped,
             stepped,
             stepped,
             stepped,
             stepped,
-            pltpu.VMEM((3, RUNS, local_len + 8, 128), F32),
-            pltpu.VMEM((RUNS, local_len, 128), F32),
+            pltpu.VMEM((3, RUNS, steps + RIM, SUB, 128), F32),
+            pltpu.VMEM((RUNS, MODES, steps, SUB, 128), F32),
             pltpu.VMEM((3, TAPS, channels), F32),
             pltpu.VMEM((6, own, MODES), F32),
             pltpu.VMEM((4, 128, 128), F32),
@@ -750,10 +776,10 @@
             pltpu.VMEM((RUNS, MODES, 128), F32),
             pltpu.VMEM((2, MODES + 8, 128), F32),
             pltpu.VMEM((2, MODES + 8, 128), F32),
-            pltpu.VMEM((2, 2 * MODES, 128), F32),
-            pltpu.VMEM((2, 2 * MODES, 128), F32),
-            pltpu.VMEM((16, 128), F32),
-            pltpu.VMEM((HALF, 16, 128), F32),
+            pltpu.VMEM((16 + 2 * MODES, 128), F32),
+            pltpu.VMEM((16 + 2 * MODES, 128), F32),
+            pltpu.VMEM((9, 128), F32),
+            pltpu.VMEM((HALF, 9, 128), F32),
             pltpu.VMEM((MODES, SUB, 128), F32),
             pltpu.VMEM((MODES, SUB, 128), F32),
             pltpu.SemaphoreType.DMA((12,)),
@@ -771,7 +797,16 @@
         residues,
         skip_weight.reshape(1, -1),
     )
-    output, grad_projected, grad_short, grad_res, grad_dec, grad_skip = results
+    output, grad_projected, grad_short, grad_res, grad_dec, grad_skip = pl.pallas_call(
+        write_out,
+        out_shape=(
+            jax.ShapeDtypeStruct(blocks, BF16),
+            jax.ShapeDtypeStruct((3,) + blocks, BF16),
+        )
+        + small,
+        in_specs=[vmem] * 5,
+        out_specs=(vmem,) * 6,
+    )(*results)
     return (
         output.reshape(channels, local_len),
         grad_projected.reshape(3, channels, local_len),

time: 43.9 us -> 35.9 us (0.82)
  local copies, waits for them, and re-layouts: 5.92 us -> 0 us
  Pallas kernels: 37 us -> 35.1 us
    unnamed x14 -> x0, local copies, waits for them, and re-layouts: 5.92 us -> none
    pallas_call x1, Pallas kernels: 37 us -> 33.2 us  [per_device(): pl.pallas_call(functools.partial(kernel, n, local_len, own), out_shape=(j...]
    pallas_call x0 -> x1, Pallas kernels: none -> 1.9 us  [per_device(): pl.pallas_call(write_out, out_shape=(jax.ShapeDtypeStruct(blocks, BF16),...]
where the time goes in v3:
time: 35.9 us; the launch traced here: 35.7 us
  Pallas kernels  35.1 us (98%)
  between operations  0.64 us (2%)
    pallas_call x1, Pallas kernels, per_device(): pl.pallas_call(functools.partial(kernel, n, local_len, own), out_shape=(j...  33.2 us
    pallas_call x1, Pallas kernels, per_device(): pl.pallas_call(write_out, out_shape=(jax.ShapeDtypeStruct(blocks, BF16),...  1.9 us

profile of v3, /device:TPU:1, one launch (start us, length us, event | category | flops | bytes accessed | tf_op | source)
XLA Modules:
  0.0 35.7 jit_solution(8743736289301542648)
XLA Ops:
  0.6 33.2 %shard_map.109 = (bf16[4,4,2,4,16,128]{5,4,3,2,1,0:T(8,128)(2,1)}, f32[3,3,512]{2,1,0:T(4,128)}, f32[16,16]{1,0:T(8,128)}, f32[16,16]{1,0:T(8,128)}, f32[1,16]{1,0:T(1,128)}) custom-call(bf16[3,4,2,4,16,128]{5,4,3,2,1,0:T(8,128)(2,1)} %bitcast.8, bf16[4,2,4,16,128]{4,3,2,1,0:T(8,128)(2,1)} %bitcast.9, f32[3,3,512]{2,1,0:T(4,128)} %bitcast.10, ...), custom_call_target="tpu_custom_call" | custom-call | tf_op jit(solution)/shard_map/pallas_call | solution.py:751
  33.8 1.9 %shard_map.110 = (bf16[4,2,4,16,128]{4,3,2,1,0:T(8,128)(2,1)}, bf16[3,4,2,4,16,128]{5,4,3,2,1,0:T(8,128)(2,1)}, f32[3,3,512]{2,1,0:T(4,128)}, f32[16,16]{1,0:T(8...) custom-call(bf16[4,4,2,4,16,128]{5,4,3,2,1,0:T(8,128)(2,1)} %get-tuple-element.17.paths, f32[3,3,512]{2,1,0:T(4,128)} %get-tuple-element.18.short, ...), custom_call_target="tpu_custom_call" | custom-call | tf_op jit(solution)/shard_map/pallas_call | solution.py:800

commit v4 on v3

--- a/solution.py
+++ b/solution.py
@@ -41,11 +41,11 @@
     decay_hbm,
     res_hbm,
     skip_hbm,
-    out_ref,
-    gshort_ref,
-    gres_ref,
-    gdec_ref,
-    gskip_ref,
+    land,
+    all_short,
+    gres_hbm,
+    gdec_hbm,
+    gskip_hbm,
     rx,
     so,
     xt,
@@ -71,7 +71,8 @@
     sums,
     sums_in,
     shorts,
-    all_short,
+    gres,
+    gskip,
     pacc,
     racc,
     send_sem,
@@ -240,7 +241,7 @@
     order = jnp.where(column == lax.rem(row, SUB) * steps + row // SUB, 1.0, 0.0).astype(BF16)
 
     def turn(arrays):
-        def tile(jt, carry):
+        def tile(jt):
             for a in arrays:
                 block = rx[pl.ds(WIDE * jt, WIDE), a].reshape(128, local_len)
                 rows = lax.dot_general(
@@ -252,9 +253,9 @@
                         moved = pltpu.roll(rows[steps - RIM + i], 1, 0)
                         first = jnp.where(group == 0, 0.0, pltpu.roll(moved, chans, 1))
                         xt[a, jt, i] = jnp.where(sub_row == 0, first, moved)
-            return carry
-
-        lax.fori_loop(0, RUNS, tile, 0)
+
+        for jt in range(RUNS):
+            tile(jt)
 
     def turn_back(rows):
         flat = rows.astype(BF16).reshape(local_len, 128)
@@ -536,7 +537,7 @@
             def _():
                 remote(
                     so.at[slot, arrays],
-                    out_ref.at[arrays, my_x, :, my_w],
+                    land.at[my_slot, arrays],
                     k,
                     (2 * jt + side) * WIDE + w,
                 ).start()
@@ -632,8 +633,8 @@
         return carry
 
     lax.fori_loop(0, RUNS, last_results, 0)
-    keep_out = pltpu.make_async_copy(so.at[my_slot], out_ref.at[:, my_x, :, my_w], local_sem.at[0])
-    keep_out.start()
+    keep_out = [pltpu.make_async_copy(so.at[my_slot], land.at[my_slot], local_sem.at[0])]
+    keep_out[0].start()
 
     pacc[...] = jnp.zeros_like(pacc)
     racc[...] = jnp.zeros_like(racc)
@@ -684,8 +685,7 @@
     each_peer(
         lambda slot, x, w, device: remote(shorts, all_short.at[my_slot], 9, device).start()
     )
-    all_short[my_slot] = shorts[...]
-    gskip_ref[...] = jnp.where(is_a, short[9:10, 0:own], short[9:10, own : 2 * own])
+    gskip[...] = jnp.where(is_a, short[9:10, 0:own], short[9:10, own : 2 * own])
 
     arrived(sums_in.at[pl.ds(16, 2 * MODES)], 11)
     plain = my_plain + sums_in[16 : 16 + MODES, :]
@@ -694,19 +694,23 @@
     grad_dec = residue * (jnp.exp(-2.0 * per) / scale * plain - scale * ramped) / (length * root)
     par[0, 0:MODES, :] = grad_res
     par[1, 0:MODES, :] = grad_dec
-    for k, ref in ((0, gres_ref), (1, gdec_ref)):
+    for k in range(2):
         turned = par[k].T
-        ref[...] = jnp.where(is_a, turned[0:own, 0:MODES], turned[own : 2 * own, 0:MODES])
+        gres[k] = jnp.where(is_a, turned[0:own, 0:MODES], turned[own : 2 * own, 0:MODES])
+    for at, (src, dst) in enumerate(
+        (
+            (shorts, all_short.at[my_slot]),
+            (gres.at[0], gres_hbm),
+            (gres.at[1], gdec_hbm),
+            (gskip, gskip_hbm),
+        )
+    ):
+        keep_out.append(pltpu.make_async_copy(src, dst, local_sem.at[1 + at]))
+        keep_out[-1].start()
 
     arrived(all_short.at[pl.ds(0, HALF - 1)], 9)
-    for jt in range(RUNS):
-        total = all_short[WIDE * jt]
-        for w in range(1, WIDE):
-            total = total + all_short[WIDE * jt + w]
-        for i in range(3):
-            gshort_ref[i, :, 128 * jt : 128 * (jt + 1)] = total[TAPS * i : TAPS * (i + 1), :]
-
-    keep_out.wait()
+    for copy in keep_out:
+        copy.wait()
     most = pl.ds(0, HALF - 1)
     arrived(so.at[most, pl.ds(0, 2)], 7)
     arrived(so.at[most, pl.ds(2, 2)], 8)
@@ -724,10 +728,18 @@
     left(all_short.at[most], 9)
 
 
-def write_out(paths, short, res, dec, skip, out, gproj, gshort, gres, gdec, gskip):
-    out[...] = paths[0]
-    gproj[...] = paths[1:]
-    gshort[...] = short[...]
+def write_out(land, parts, res, dec, skip, out, gproj, gshort, gres, gdec, gskip):
+    for x in range(RUNS):
+        for half in range(2):
+            for w in range(WIDE):
+                out[x, half, w] = land[WIDE * x + w, 0, half]
+                for a in range(3):
+                    gproj[a, x, half, w] = land[WIDE * x + w, 1 + a, half]
+        total = parts[WIDE * x]
+        for w in range(1, WIDE):
+            total = total + parts[WIDE * x + w]
+        for i in range(3):
+            gshort[i, :, 128 * x : 128 * (x + 1)] = total[TAPS * i : TAPS * (i + 1), :]
     gres[...] = res[...]
     gdec[...] = dec[...]
     gskip[...] = skip[...]
@@ -743,16 +755,19 @@
     stepped = pltpu.VMEM((RUNS, steps, SUB, 128), F32)
     blocks = (RUNS, 2, WIDE, own, local_len)
     small = (
-        jax.ShapeDtypeStruct((3, TAPS, channels), F32),
         jax.ShapeDtypeStruct((own, MODES), F32),
         jax.ShapeDtypeStruct((own, MODES), F32),
         jax.ShapeDtypeStruct((1, own), F32),
     )
     results = pl.pallas_call(
         functools.partial(kernel, n, local_len, own),
-        out_shape=(jax.ShapeDtypeStruct((4,) + blocks, BF16),) + small,
+        out_shape=(
+            jax.ShapeDtypeStruct((HALF, 4, 2, own, local_len), BF16),
+            jax.ShapeDtypeStruct((HALF, 3 * TAPS, 128), F32),
+        )
+        + small,
         in_specs=[hbm] * 6,
-        out_specs=(vmem,) * 5,
+        out_specs=(hbm,) * 5,
         scratch_shapes=[
             pltpu.VMEM((HALF, 4, 2, own, local_len), BF16),
             pltpu.VMEM((HALF, 4, 2, own, local_len), BF16),
@@ -779,7 +794,8 @@
             pltpu.VMEM((16 + 2 * MODES, 128), F32),
             pltpu.VMEM((16 + 2 * MODES, 128), F32),
             pltpu.VMEM((9, 128), F32),
-            pltpu.VMEM((HALF, 9, 128), F32),
+            pltpu.VMEM((2, own, MODES), F32),
+            pltpu.VMEM((1, own), F32),
             pltpu.VMEM((MODES, SUB, 128), F32),
             pltpu.VMEM((MODES, SUB, 128), F32),
             pltpu.SemaphoreType.DMA((12,)),
@@ -802,6 +818,7 @@
         out_shape=(
             jax.ShapeDtypeStruct(blocks, BF16),
             jax.ShapeDtypeStruct((3,) + blocks, BF16),
+            jax.ShapeDtypeStruct((3, TAPS, channels), F32),
         )
         + small,
         in_specs=[vmem] * 5,

time: 35.9 us -> 34.7 us (0.967)
  Pallas kernels: 35.1 us -> 33.8 us
    pallas_call x1, Pallas kernels: 33.2 us -> 31.9 us  [per_device(): pl.pallas_call(functools.partial(kernel, n, local_len, own), out_shape=(j...]
where the time goes in v4:
time: 34.7 us; the launch traced here: 34.5 us
  Pallas kernels  33.8 us (97%)
  between operations  0.64 us (2%)
    pallas_call x1, Pallas kernels, per_device(): pl.pallas_call(functools.partial(kernel, n, local_len, own), out_shape=(j...  31.9 us
    pallas_call x1, Pallas kernels, per_device(): pl.pallas_call(write_out, out_shape=(jax.ShapeDtypeStruct(blocks, BF16),...  1.96 us

profile of v4, /device:TPU:1, one launch (start us, length us, event | category | flops | bytes accessed | tf_op | source)
XLA Modules:
  0.0 34.5 jit_solution(11360815960633105220)
XLA Ops:
  0.6 31.9 %shard_map.109 = (bf16[16,4,2,16,128]{4,3,2,1,0:T(8,128)(2,1)}, f32[16,9,128]{2,1,0:T(8,128)}, f32[16,16]{1,0:T(8,128)}, f32[16,16]{1,0:T(8,128)}, f32[1,16]{1,0:T(1,128)}) custom-call(bf16[3,4,2,4,16,128]{5,4,3,2,1,0:T(8,128)(2,1)} %bitcast.8, bf16[4,2,4,16,128]{4,3,2,1,0:T(8,128)(2,1)} %bitcast.9, f32[3,3,512]{2,1,0:T(4,128)} %bitcast.10, ...), custom_call_target="tpu_custom_call" | custom-call | tf_op jit(solution)/shard_map/pallas_call | solution.py:762
  32.5 2.0 %shard_map.110 = (bf16[4,2,4,16,128]{4,3,2,1,0:T(8,128)(2,1)}, bf16[3,4,2,4,16,128]{5,4,3,2,1,0:T(8,128)(2,1)}, f32[3,3,512]{2,1,0:T(4,128)}, f32[16,16]{1,0:T(8...) custom-call(bf16[16,4,2,16,128]{4,3,2,1,0:T(8,128)(2,1)} %get-tuple-element.17.land, f32[16,9,128]{2,1,0:T(8,128)} %get-tuple-element.18.parts, ...), custom_call_target="tpu_custom_call" | custom-call | tf_op jit(solution)/shard_map/pallas_call | solution.py:816

commit v5 on v4

--- a/solution.py
+++ b/solution.py
@@ -614,18 +614,28 @@
         0, RUNS, back_tile, tuple(jnp.zeros((SUB, 128), F32) for _ in range(10))
     )
 
-    rows = jnp.concatenate(
-        [jnp.sum(part, axis=0, keepdims=True) for part in found] + [jnp.zeros((6, 128), F32)],
-        axis=0,
-    )
-    my_short = group_sum(rows) * (1.0 / root)
-    sums[0:16, :] = my_short
-    remote(sums.at[pl.ds(0, 16)], sums_in.at[pl.ds(0, 16)], 6, partner).start()
+    taps = [group_sum(jnp.sum(part, axis=0, keepdims=True)) * (1.0 / root) for part in found]
+    sides = []
+    for r in range(3):
+        side_row = jnp.zeros((1, 128), F32)
+        for g in range(4):
+            if 4 * r + g < 3 * TAPS:
+                side_row = jnp.where(group == g, taps[4 * r + g], side_row)
+        sides.append(side_row)
+    shorts[...] = jnp.concatenate(sides + [jnp.zeros((1, 128), F32)], axis=0)
+
+    def send_short(t, carry):
+        remote(shorts, all_short.at[me], 9, lax.rem(me + t, n)).start()
+        return carry
 
     gf_rim(1)
     gf_rim(2)
 
     def last_results(t, carry):
+        @pl.when(t < 2)
+        def _():
+            lax.fori_loop(jnp.maximum(16 * t, 1), 16 * t + 16, send_short, 0)
+
         jt = lax.rem(my_x + 1 + t, RUNS)
         grad_path(1, jt)
         grad_path(2, jt)
@@ -668,28 +678,16 @@
     my_ramped = group_sum(
         jnp.concatenate([jnp.sum(racc[m], axis=0, keepdims=True) for m in range(MODES)], axis=0)
     )
-    sums[16 : 16 + MODES, :] = my_plain
-    sums[16 + MODES : 16 + 2 * MODES, :] = my_ramped
-    remote(
-        sums.at[pl.ds(16, 2 * MODES)], sums_in.at[pl.ds(16, 2 * MODES)], 11, partner
-    ).start()
-
-    arrived(sums_in.at[pl.ds(0, 16)], 6)
-    short = my_short + sums_in[0:16, :]
-    odd = lax.rem(my_w, 2) == 1
-    other = pltpu.roll(short, own, 1)
-    low = jnp.where(odd, other, short)[0:9, :]
-    high = jnp.where(odd, short, other)[0:9, :]
-    place = lane // own
-    shorts[...] = jnp.where(place == my_w, low, jnp.where(place == my_w + WIDE, high, 0.0))
-    each_peer(
-        lambda slot, x, w, device: remote(shorts, all_short.at[my_slot], 9, device).start()
-    )
-    gskip[...] = jnp.where(is_a, short[9:10, 0:own], short[9:10, own : 2 * own])
-
-    arrived(sums_in.at[pl.ds(16, 2 * MODES)], 11)
-    plain = my_plain + sums_in[16 : 16 + MODES, :]
-    ramped = lam_rows * (my_ramped + sums_in[16 + MODES : 16 + 2 * MODES, :])
+    sums[0:MODES, :] = my_plain
+    sums[MODES : 2 * MODES, :] = my_ramped
+    sums[2 * MODES : 2 * MODES + 8, :] = jnp.broadcast_to(taps[9], (SUB, 128))
+    remote(sums, sums_in, 6, partner).start()
+
+    arrived(sums_in, 6)
+    plain = my_plain + sums_in[0:MODES, :]
+    ramped = lam_rows * (my_ramped + sums_in[MODES : 2 * MODES, :])
+    skips = taps[9] + sums_in[2 * MODES : 2 * MODES + 1, :]
+    gskip[...] = jnp.where(is_a, skips[:, 0:own], skips[:, own : 2 * own])
     grad_res = scale * plain / root
     grad_dec = residue * (jnp.exp(-2.0 * per) / scale * plain - scale * ramped) / (length * root)
     par[0, 0:MODES, :] = grad_res
@@ -699,7 +697,7 @@
         gres[k] = jnp.where(is_a, turned[0:own, 0:MODES], turned[own : 2 * own, 0:MODES])
     for at, (src, dst) in enumerate(
         (
-            (shorts, all_short.at[my_slot]),
+            (shorts, all_short.at[me]),
             (gres.at[0], gres_hbm),
             (gres.at[1], gdec_hbm),
             (gskip, gskip_hbm),
@@ -708,7 +706,7 @@
         keep_out.append(pltpu.make_async_copy(src, dst, local_sem.at[1 + at]))
         keep_out[-1].start()
 
-    arrived(all_short.at[pl.ds(0, HALF - 1)], 9)
+    arrived(all_short.at[pl.ds(0, n - 1)], 9)
     for copy in keep_out:
         copy.wait()
     most = pl.ds(0, HALF - 1)
@@ -721,25 +719,35 @@
     left(edge.at[0], 4)
     left(edge.at[1, pl.ds(0, MODES)], 5)
     left(edge.at[1, pl.ds(MODES, 8)], 10)
-    left(sums.at[pl.ds(0, 16)], 6)
-    left(sums.at[pl.ds(16, 2 * MODES)], 11)
+    left(sums, 6)
     left(so.at[most, pl.ds(0, 2)], 7)
     left(so.at[most, pl.ds(2, 2)], 8)
-    left(all_short.at[most], 9)
+    left(all_short.at[pl.ds(0, n - 1)], 9)
 
 
 def write_out(land, parts, res, dec, skip, out, gproj, gshort, gres, gdec, gskip):
+    own = land.shape[3]
+    place = lax.broadcasted_iota(jnp.int32, (1, 128), 1) // own
     for x in range(RUNS):
         for half in range(2):
             for w in range(WIDE):
                 out[x, half, w] = land[WIDE * x + w, 0, half]
                 for a in range(3):
                     gproj[a, x, half, w] = land[WIDE * x + w, 1 + a, half]
-        total = parts[WIDE * x]
-        for w in range(1, WIDE):
-            total = total + parts[WIDE * x + w]
-        for i in range(3):
-            gshort[i, :, 128 * x : 128 * (x + 1)] = total[TAPS * i : TAPS * (i + 1), :]
+        rows = [jnp.zeros((4, 128), F32) for _ in range(4)]
+        for w in range(WIDE):
+            at = 2 * WIDE * x + w
+            both = parts[at] + parts[at + WIDE]
+            for g in range(4):
+                low = (own * w - 2 * own * g) % 128
+                high = (64 + own * w - own - 2 * own * g) % 128
+                low = pltpu.roll(both, low, 1) if low else both
+                high = pltpu.roll(both, high, 1) if high else both
+                rows[g] = jnp.where(place == w, low, jnp.where(place == w + WIDE, high, rows[g]))
+        for k in range(3 * TAPS):
+            gshort[k // TAPS, k % TAPS : k % TAPS + 1, 128 * x : 128 * (x + 1)] = rows[k % 4][
+                k // 4 : k // 4 + 1, :
+            ]
     gres[...] = res[...]
     gdec[...] = dec[...]
     gskip[...] = skip[...]
@@ -763,7 +771,7 @@
         functools.partial(kernel, n, local_len, own),
         out_shape=(
             jax.ShapeDtypeStruct((HALF, 4, 2, own, local_len), BF16),
-            jax.ShapeDtypeStruct((HALF, 3 * TAPS, 128), F32),
+            jax.ShapeDtypeStruct((n, 4, 128), F32),
         )
         + small,
         in_specs=[hbm] * 6,
@@ -791,15 +799,15 @@
             pltpu.VMEM((RUNS, MODES, 128), F32),
             pltpu.VMEM((2, MODES + 8, 128), F32),
             pltpu.VMEM((2, MODES + 8, 128), F32),
-            pltpu.VMEM((16 + 2 * MODES, 128), F32),
-            pltpu.VMEM((16 + 2 * MODES, 128), F32),
-            pltpu.VMEM((9, 128), F32),
+            pltpu.VMEM((8 + 2 * MODES, 128), F32),
+            pltpu.VMEM((8 + 2 * MODES, 128), F32),
+            pltpu.VMEM((4, 128), F32),
             pltpu.VMEM((2, own, MODES), F32),
             pltpu.VMEM((1, own), F32),
             pltpu.VMEM((MODES, SUB, 128), F32),
             pltpu.VMEM((MODES, SUB, 128), F32),
-            pltpu.SemaphoreType.DMA((12,)),
-            pltpu.SemaphoreType.DMA((12,)),
+            pltpu.SemaphoreType.DMA((11,)),
+            pltpu.SemaphoreType.DMA((11,)),
             pltpu.SemaphoreType.DMA((6,)),
         ],
         compiler_params=pltpu.CompilerParams(

time: 34.7 us -> 33.4 us (0.963)
  Pallas kernels: 33.8 us -> 32.6 us
    pallas_call x1, Pallas kernels: 31.9 us -> 30.6 us  [per_device(): pl.pallas_call(functools.partial(kernel, n, local_len, own), out_shape=(j...]
where the time goes in v5:
time: 33.4 us; the launch traced here: 33.2 us
  Pallas kernels  32.6 us (98%)
  between operations  0.64 us (2%)
    pallas_call x1, Pallas kernels, per_device(): pl.pallas_call(functools.partial(kernel, n, local_len, own), out_shape=(j...  30.6 us
    pallas_call x1, Pallas kernels, per_device(): pl.pallas_call(write_out, out_shape=(jax.ShapeDtypeStruct(blocks, BF16),...  2.04 us

profile of v5, /device:TPU:1, one launch (start us, length us, event | category | flops | bytes accessed | tf_op | source)
XLA Modules:
  0.0 33.2 jit_solution(16269954376985723127)
XLA Ops:
  0.6 30.6 %shard_map.109 = (bf16[16,4,2,16,128]{4,3,2,1,0:T(8,128)(2,1)}, f32[32,4,128]{2,1,0:T(4,128)}, f32[16,16]{1,0:T(8,128)}, f32[16,16]{1,0:T(8,128)}, f32[1,16]{1,0:T(1,128)}) custom-call(bf16[3,4,2,4,16,128]{5,4,3,2,1,0:T(8,128)(2,1)} %bitcast.8, bf16[4,2,4,16,128]{4,3,2,1,0:T(8,128)(2,1)} %bitcast.9, f32[3,3,512]{2,1,0:T(4,128)} %bitcast.10, ...), custom_call_target="tpu_custom_call" | custom-call | tf_op jit(solution)/shard_map/pallas_call | solution.py:770
  31.2 2.0 %shard_map.110 = (bf16[4,2,4,16,128]{4,3,2,1,0:T(8,128)(2,1)}, bf16[3,4,2,4,16,128]{5,4,3,2,1,0:T(8,128)(2,1)}, f32[3,3,512]{2,1,0:T(4,128)}, f32[16,16]{1,0:T(8...) custom-call(bf16[16,4,2,16,128]{4,3,2,1,0:T(8,128)(2,1)} %get-tuple-element.17.land, f32[32,4,128]{2,1,0:T(4,128)} %get-tuple-element.18.parts, ...), custom_call_target="tpu_custom_call" | custom-call | tf_op jit(solution)/shard_map/pallas_call | solution.py:824

commit v6 on v5

--- a/solution.py
+++ b/solution.py
@@ -35,8 +35,8 @@
     n,
     local_len,
     own,
-    proj_ref,
-    cot_ref,
+    proj_hbm,
+    cot_hbm,
     sw_hbm,
     decay_hbm,
     res_hbm,
@@ -46,6 +46,8 @@
     gres_hbm,
     gdec_hbm,
     gskip_hbm,
+    proj_ref,
+    cot_ref,
     rx,
     so,
     xt,
@@ -136,7 +138,11 @@
         ),
         pltpu.make_async_copy(cot_ref.at[my_x, :, my_w], rx.at[my_slot, 3], local_sem.at[5]),
     ]
-    for copy in small + keep:
+    whole = [
+        pltpu.make_async_copy(proj_hbm, proj_ref, local_sem.at[6]),
+        pltpu.make_async_copy(cot_hbm, cot_ref, local_sem.at[7]),
+    ]
+    for copy in whole + small:
         copy.start()
 
     lane = lax.broadcasted_iota(jnp.int32, (1, 128), 1)
@@ -171,6 +177,10 @@
     def after(rows):
         return jnp.where(group < RUNS - 1, pltpu.roll(rows, 128 - chans, 1), 0.0)
 
+    for copy in whole:
+        copy.wait()
+    for copy in keep:
+        copy.start()
     for copy in small:
         copy.wait()
     pl.semaphore_wait(barrier, HALF)
@@ -425,7 +435,8 @@
             us[jt, p] = rounded(key * value)
         return carry
 
-    lax.fori_loop(0, RUNS, regate_kv, 0)
+    for jt in range(RUNS):
+        regate_kv(jt, 0)
     my_k = edge_path(1, k_first, theirs_before(tk_last))
     my_v = edge_path(2, v_first, theirs_before(tv_last))
     their_k = edge_path(1, tk_first, mine_before(k_last))
@@ -499,7 +510,8 @@
             gf[0, jt, p] = xt[3, jt, RIM + p] * cv[jt, p]
         return carry
 
-    lax.fori_loop(0, RUNS, regate_q, 0)
+    for jt in range(RUNS):
+        regate_q(jt, 0)
     next_u = [theirs_after(u) for u in their_u]
     next_c = theirs_after(tc_first)
     state0 = lam_rows * next_f + next_u[0]
@@ -553,7 +565,8 @@
         send_tile(jt, pl.ds(0, 2), 7)
         return carry
 
-    lax.fori_loop(0, RUNS, first_results, 0)
+    for t in range(RUNS):
+        first_results(t, 0)
 
     my_q = edge_path(0, q_first, theirs_before(tq_last))
     their_q = edge_path(0, tq_first, mine_before(q_last))
@@ -777,6 +790,8 @@
         in_specs=[hbm] * 6,
         out_specs=(hbm,) * 5,
         scratch_shapes=[
+            pltpu.VMEM((3,) + blocks, BF16),
+            pltpu.VMEM(blocks, BF16),
             pltpu.VMEM((HALF, 4, 2, own, local_len), BF16),
             pltpu.VMEM((HALF, 4, 2, own, local_len), BF16),
             pltpu.VMEM((4, RUNS, RIM + steps, SUB, 128), F32),
@@ -808,7 +823,7 @@
             pltpu.VMEM((MODES, SUB, 128), F32),
             pltpu.SemaphoreType.DMA((11,)),
             pltpu.SemaphoreType.DMA((11,)),
-            pltpu.SemaphoreType.DMA((6,)),
+            pltpu.SemaphoreType.DMA((8,)),
         ],
         compiler_params=pltpu.CompilerParams(
             collective_id=0, has_side_effects=True, vmem_limit_bytes=56 * 1024 * 1024

time: 33.4 us -> 33 us (0.988)
  Pallas kernels: 32.6 us -> 32.2 us
    pallas_call x1, Pallas kernels: 30.6 us -> 30.2 us  [per_device(): pl.pallas_call(functools.partial(kernel, n, local_len, own), out_shape=(j...]
where the time goes in v6:
time: 33 us; the launch traced here: 32.8 us
  Pallas kernels  32.2 us (98%)
  between operations  0.64 us (2%)
    pallas_call x1, Pallas kernels, per_device(): pl.pallas_call(functools.partial(kernel, n, local_len, own), out_shape=(j...  30.2 us
    pallas_call x1, Pallas kernels, per_device(): pl.pallas_call(write_out, out_shape=(jax.ShapeDtypeStruct(blocks, BF16),...  2.04 us

profile of v6, /device:TPU:1, one launch (start us, length us, event | category | flops | bytes accessed | tf_op | source)
XLA Modules:
  0.0 32.8 jit_solution(6468735544203007452)
XLA Ops:
  0.6 30.2 %shard_map.109 = (bf16[16,4,2,16,128]{4,3,2,1,0:T(8,128)(2,1)}, f32[32,4,128]{2,1,0:T(4,128)}, f32[16,16]{1,0:T(8,128)}, f32[16,16]{1,0:T(8,128)}, f32[1,16]{1,0:T(1,128)}) custom-call(bf16[3,4,2,4,16,128]{5,4,3,2,1,0:T(8,128)(2,1)} %bitcast.8, bf16[4,2,4,16,128]{4,3,2,1,0:T(8,128)(2,1)} %bitcast.9, f32[3,3,512]{2,1,0:T(4,128)} %bitcast.10, ...), custom_call_target="tpu_custom_call" | custom-call | tf_op jit(solution)/shard_map/pallas_call | solution.py:783
  30.8 2.0 %shard_map.110 = (bf16[4,2,4,16,128]{4,3,2,1,0:T(8,128)(2,1)}, bf16[3,4,2,4,16,128]{5,4,3,2,1,0:T(8,128)(2,1)}, f32[3,3,512]{2,1,0:T(4,128)}, f32[16,16]{1,0:T(8...) custom-call(bf16[16,4,2,16,128]{4,3,2,1,0:T(8,128)(2,1)} %get-tuple-element.17.land, f32[32,4,128]{2,1,0:T(4,128)} %get-tuple-element.18.parts, ...), custom_call_target="tpu_custom_call" | custom-call | tf_op jit(solution)/shard_map/pallas_call | solution.py:839
